TPU v7x, 512 devices: a whole 4x4x16 slice. The times are simulated.
512 devices in a mesh: grp: 16 (over x_lo, y, core), row: 32 (over z, x_hi).
Axes of the slice: x: 4 (x_hi: 2, x_lo: 2; x = x_hi * 2 + x_lo), y: 4, z: 16, core: 2. Of those that a mesh axis runs over, the one named last changes fastest.
Arguments:
- snapshots: float32 [8192, 8192], P('row', 'grp'), may hold values from -200 to 200
Outputs:
- rotated: float32 [8192, 8192], P('row', 'grp')
All inputs are finite; a program needn't handle non-finite values.
Results may differ from a plain program's by a relative error of at most 0.0003.
Values sent between devices are 32-bit elements; how exact they have to be, the bound alone decides.
No kernel may reach another device: no remote copies, remote signals or barrier semaphores. Data moves between devices by JAX's collectives and lax.ppermute only.
A program may use at most 64 MiB of HBM per device.

v0:
```python
import functools

import jax
import jax.numpy as jnp
from jax import lax
from jax.experimental import pallas as pl
from jax.experimental.pallas import tpu as pltpu
from jax.sharding import Mesh
from jax.sharding import PartitionSpec as P

ROUNDS = 6
HALF = 256
REACH = 10
EDGE = 32
DIAGS = 24
MID = 12
LINES = 28

f32 = jnp.float32
INTERPRET = False


def lanes(shape):
    return lax.broadcasted_iota(jnp.int32, shape, 1)


def turn_lanes(x, by):
    by %= x.shape[1]
    return pltpu.roll(x, by, axis=1) if by else x


def turn_lines(x, by):
    return pltpu.roll(x, by % x.shape[0], axis=0)


def mirrored(x):
    n = x.shape[1]
    row = lax.broadcasted_iota(jnp.int32, (n, n), 0)
    flip = jnp.where(row + lanes((n, n)) == n - 1, 1.0, 0.0).astype(jnp.bfloat16)
    high = x.astype(jnp.bfloat16)
    rest = x - high.astype(f32)
    middle = rest.astype(jnp.bfloat16)
    low = (rest - middle.astype(f32)).astype(jnp.bfloat16)
    dot = functools.partial(jnp.dot, preferred_element_type=f32)
    return (dot(low, flip) + dot(middle, flip)) + dot(high, flip)


def ends(t, b):
    t0, t1, b0, b1 = t[:, :128], t[:, 128:], b[:, :128], b[:, 128:]
    at = lanes(t0.shape)
    return jnp.where(
        at < 32, t0, jnp.where(at < 64, turn_lanes(t1, 64), jnp.where(at < 96, turn_lanes(b0, 64), b1))
    )


def band_of(t_ref, b_ref, out_ref):
    count = t_ref.shape[0] // 8

    def same(k, sums):
        at = pl.ds(pl.multiple_of(k * 8, 8), 8)
        t, b = t_ref[at, :], b_ref[at, :]
        new = []
        for j in range(6):
            new.append(sums[j] + t * turn_lanes(t, -2 * j))
        for j in range(6):
            new.append(sums[6 + j] + b * turn_lanes(b, -2 * j))
        return tuple(new)

    def cross(k, sums):
        at = pl.ds(pl.multiple_of(k * 8, 8), 8)
        t, b = t_ref[at, :], b_ref[at, :]
        new = []
        for j in range(6):
            new.append(sums[j] + t * turn_lanes(b, -2 * j))
        for j in range(1, 6):
            new.append(sums[5 + j] + b * turn_lanes(t, -2 * j))
        e = ends(t, b)
        swapped = turn_lanes(e, 64)
        for j in range(5):
            new.append(sums[11 + j] + e * turn_lanes(e, -2 * j - 1))
        for j in range(5):
            new.append(sums[16 + j] + e * turn_lanes(swapped, -2 * j - 1))
        return tuple(new)

    wide, narrow = jnp.zeros((8, 256), f32), jnp.zeros((8, 128), f32)
    first = lax.fori_loop(0, count, same, (wide,) * 12)
    second = lax.fori_loop(0, count, cross, (wide,) * 11 + (narrow,) * 10)

    def put(line, value):
        for k in range(out_ref.shape[0]):
            out_ref[k, line : line + 1, :] = value

    for line, value in enumerate(first + second[:11]):
        total = jnp.sum(value, axis=0, keepdims=True)
        put(line, total[:, :128])
        put(LINES + line, total[:, 128:])
    for j in range(5):
        put(23 + j, jnp.sum(second[11 + j], axis=0, keepdims=True))
        put(LINES + 23 + j, jnp.sum(second[16 + j], axis=0, keepdims=True))


def spread(e, top):
    both = jnp.concatenate([e, e], axis=1)
    at = lanes(both.shape)
    first, last = (both, turn_lanes(both, 64)) if top else (turn_lanes(both, -64), both)
    return jnp.where(at < EDGE, first, jnp.where(at >= HALF - EDGE, last, 0.0))


def along_columns(x):
    shifted = jnp.broadcast_to(turn_lanes(x, -MID), (DIAGS, HALF))
    return pltpu.roll(shifted, 0, axis=1, stride=1, stride_axis=0)


def angles_of(parts_ref, x_ref):
    band = parts_ref[0]
    for k in range(1, parts_ref.shape[0]):
        band = band + parts_ref[k]
    low, high = band[:LINES], band[LINES:]
    blank = jnp.zeros((1, HALF), f32)
    for block in range(4):
        for line in (0, DIAGS - 2, DIAGS - 1):
            x_ref[block, line : line + 1, :] = blank
    TT, TB, BT, BB = 0, 1, 2, 3

    def put(block, other, d, value):
        x_ref[block, MID - d : MID - d + 1, :] = value
        x_ref[other, MID + d : MID + d + 1, :] = turn_lanes(value, d)

    def line(k):
        return jnp.concatenate([low[k : k + 1], high[k : k + 1]], axis=1)

    for j in range(6):
        put(TT, TT, 2 * j, line(j))
        put(BB, BB, 2 * j, line(6 + j))
        put(TB, BT, 2 * j, line(12 + j))
        if j:
            put(BT, TB, 2 * j, line(17 + j))
    alike, across = low[23:28], high[23:28]
    odd = [
        (TT, TT, spread(alike, True)),
        (BB, BB, spread(alike, False)),
        (TB, BT, spread(across, True)),
        (BT, TB, spread(across, False)),
    ]
    for block, other, value in odd:
        for j in range(5):
            put(block, other, 2 * j + 1, value[j : j + 1])

    tt, tb, bt, bb = (x_ref[k] for k in range(4))
    shape = (DIAGS, HALF)
    i = lanes(shape)
    j = i + MID - lax.broadcasted_iota(jnp.int32, shape, 0)
    i_one, i_more, i_last = i == 1, i >= 2, i == HALF - 1
    j_one, j_more, j_last = j == 1, j >= 2, j == HALF - 1

    def less(x):
        return turn_lines(x, -1)

    def more(x):
        return turn_lines(x, 1)

    cosines, sines = [], []
    for turn in range(ROUNDS):
        first, second, coupling = (x[MID : MID + 1] for x in (tt, bb, tb))
        difference = second - first
        direction = jnp.where(difference >= 0, 1.0, -1.0)
        denominator = (
            jnp.abs(difference)
            + jnp.sqrt(difference * difference + 4.0 * coupling * coupling)
            + 1e-06 * (first + second)
        )
        tangent = direction * 2.0 * coupling / denominator
        c = 1.0 / jnp.sqrt(1.0 + tangent * tangent)
        s = tangent * c
        cosines.append(c)
        sines.append(s)
        if turn == ROUNDS - 1:
            break
        c_row, s_row = jnp.broadcast_to(c, shape), jnp.broadcast_to(s, shape)
        c_col, s_col = along_columns(c), along_columns(s)
        tt, tb = c_col * tt - s_col * tb, s_col * tt + c_col * tb
        bt, bb = c_col * bt - s_col * bb, s_col * bt + c_col * bb
        tt, bt = c_row * tt - s_row * bt, s_row * tt + c_row * bt
        tb, bb = c_row * tb - s_row * bb, s_row * tb + c_row * bb
        tt, tb = (
            jnp.where(j_more, less(tt), jnp.where(j_one, less(tb), tt)),
            jnp.where(j_last, tt, more(tb)),
        )
        bt, bb = (
            jnp.where(j_more, less(bt), jnp.where(j_one, less(bb), bt)),
            jnp.where(j_last, bt, more(bb)),
        )
        tt, bt = (
            jnp.where(i_more, turn_lanes(more(tt), 1), jnp.where(i_one, turn_lanes(more(bt), 1), tt)),
            jnp.where(i_last, tt, turn_lanes(less(bt), -1)),
        )
        tb, bb = (
            jnp.where(i_more, turn_lanes(more(tb), 1), jnp.where(i_one, turn_lanes(more(bb), 1), tb)),
            jnp.where(i_last, tb, turn_lanes(less(bb), -1)),
        )
    return cosines, sines


def turned(t, b, cosines, sines):
    at = lanes(t.shape)
    none, one, more, last = at == 0, at == 1, at >= 2, at == HALF - 1
    for turn in range(ROUNDS):
        c, s = cosines[turn], sines[turn]
        t, b = c * t - s * b, s * t + c * b
        if turn < ROUNDS - 1:
            t, b = (
                jnp.where(more, turn_lanes(t, 1), jnp.where(one, turn_lanes(b, 1), t)),
                jnp.where(last, t, turn_lanes(b, -1)),
            )
    for turn in range(ROUNDS - 1):
        t, b = (
            jnp.where(none, t, jnp.where(last, b, turn_lanes(t, -1))),
            jnp.where(none, turn_lanes(t, -1), turn_lanes(b, 1)),
        )
    return t, b


def each_chunk(t_ref, b_ref, t_out, b_out, cosines, sines, rows=16):
    shape = (rows, HALF)
    cosines = [jnp.broadcast_to(c, shape) for c in cosines]
    sines = [jnp.broadcast_to(s, shape) for s in sines]

    def chunk(k, carry):
        at = pl.ds(pl.multiple_of(k * rows, rows), rows)
        t_out[at, :], b_out[at, :] = turned(t_ref[at, :], b_ref[at, :], cosines, sines)
        return carry

    lax.fori_loop(0, t_ref.shape[0] // rows, chunk, 0)


def first_band(p_ref, out_ref, b_ref):
    b_ref[...] = mirrored(p_ref[:, HALF:])
    band_of(p_ref.at[:, :HALF], b_ref, out_ref)


def first_turn(parts_ref, p_ref, b_ref, t_out, b_out, x_ref):
    cosines, sines = angles_of(parts_ref, x_ref)
    each_chunk(p_ref.at[:, :HALF], b_ref, t_out, b_out, cosines, sines)


def second_band(t_ref, b_ref, out_ref):
    band_of(t_ref, b_ref, out_ref)


def second_turn(parts_ref, t_ref, b_ref, out_ref, x_ref, b_out):
    cosines, sines = angles_of(parts_ref, x_ref)
    each_chunk(t_ref, b_ref, out_ref.at[:, :HALF], b_out, cosines, sines)
    out_ref[:, HALF:] = mirrored(b_out[...])


def call(body, outs, args, scratch=()):
    vmem = pl.BlockSpec(memory_space=pltpu.VMEM)
    shapes = [jax.ShapeDtypeStruct(s, f32) for s in outs]
    return pl.pallas_call(
        body,
        out_shape=shapes,
        in_specs=[vmem] * len(args),
        out_specs=[vmem] * len(outs),
        scratch_shapes=[pltpu.VMEM(s, f32) for s in scratch],
        compiler_params=pltpu.CompilerParams(vmem_limit_bytes=32 * 1024 * 1024),
        interpret=INTERPRET,
    )(*args)


NEAR, FAR = ("near",), ("far", "side")


def exchanged(parts, near, far):
    arrived = lax.all_to_all(parts, NEAR, 0, 0, tiled=True)
    total = arrived[0]
    for k in range(1, near):
        total = total + arrived[k]
    again = jnp.broadcast_to(total[None], (far, *total.shape))
    return lax.all_to_all(again, FAR, 0, 0, tiled=True)


def per_device(snapshots, near, far, groups):
    rows = snapshots.shape[0]
    square, band, state = (rows, HALF), (near, 2 * LINES, 128), (4, DIAGS, HALF)
    parts, b = call(first_band, [band, square], [snapshots])
    t, b = call(first_turn, [square, square], [exchanged(parts, near, far), snapshots, b], [state])
    b = lax.ppermute(b, "grp", [(i, (i + 1) % groups) for i in range(groups)])
    (parts,) = call(second_band, [band], [t, b])
    (out,) = call(
        second_turn, [(rows, 2 * HALF)], [exchanged(parts, near, far), t, b], [state, square]
    )
    return out


def solution(mesh):
    groups, rows = mesh.shape["grp"], mesh.shape["row"]
    near, side = 4, 2
    far = rows // (near * side)
    fine = Mesh(mesh.devices.reshape(groups, far, near, side), ("grp", "far", "near", "side"))
    placed = P(("far", "near", "side"), "grp")
    body = functools.partial(per_device, near=near, far=far * side, groups=groups)
    return jax.shard_map(body, mesh=fine, in_specs=(placed,), out_specs=placed, check_vma=False)
```

profile of v0, /device:TPU:32, one launch (start us, length us, event | category | flops | bytes accessed | tf_op | source)
XLA Modules:
  0.0 133.5 jit_solution(17161584597013016533)
XLA Ops:
  0.0 0.0 copy-start
  0.0 1.0 copy-done
  1.0 10.1 %shard_map.17 = (f32[4,56,128]{2,1,0:T(8,128)S(1)}, f32[256,256]{1,0:T(8,128)S(1)}) custom-call(f32[256,512]{1,0:T(8,128)S(1)} %copy-done), custom_call_target="tpu_custom_call" | custom-call | tf_op jit(solution)/shard_map/pallas_call | solution.py:259
  11.2 12.9 %all_to_all.20 = f32[4,56,128]{2,1,0:T(8,128)S(1)} all-to-all(f32[4,56,128]{2,1,0:T(8,128)S(1)} %get-tuple-element.9), channel_id=1, replica_groups=mesh['grp'=16,'far'=4,'near'=4,'side'=2] {'near'}, dimensions={0} | all-to-all | bytes 229376 | tf_op jit(solution)/shard_map/all_to_all | solution.py:274
  24.1 30.9 %all_to_all.21.parts_ref = f32[8,56,128]{2,1,0:T(8,128)S(1)} all-to-all(f32[8,56,128]{2,1,0:T(8,128)S(1)} %broadcast_in_dim.17), channel_id=1, replica_groups=mesh['grp'=16,'far'=4,'near'=4,'side'=2] {'far','side'}, dimensions={0} | all-to-all | bytes 458752 | tf_op jit(solution)/shard_map/all_to_all | solution.py:279
  55.0 13.8 %shard_map.18 = (f32[256,256]{1,0:T(8,128)S(1)}, f32[256,256]{1,0:T(8,128)S(1)}) custom-call(f32[8,56,128]{2,1,0:T(8,128)S(1)} %all_to_all.21.parts_ref, f32[256,512]{1,0:T(8,128)S(1)} %copy-done, f32[256,256]{1,0:T(8,128)S(1)} %get-tuple-element.10.b_ref), custom_call_target="tpu_custom_call" | custom-call | tf_op jit(solution)/shard_map/pallas_call | solution.py:259
  68.8 1.9 %collective-permute-start = (f32[256,256]{1,0:T(8,128)S(1)}, f32[256,256]{1,0:T(8,128)S(1)}, u32[]{:S(2)}, u32[]{:S(2)}) collective-permute-start(f32[256,256]{1,0:T(8,128)S(1)} %get-tuple-element.12), channel_id=1, source_target_pairs={{0,32},{32,64},{64,96},{96,128},{128,160},{160,192},{192,224},{224... | collective-permute-start | bytes 786440 | tf_op jit(solution)/shard_map/ppermute | solution.py:287
  70.8 7.9 %collective-permute-done.b_ref = f32[256,256]{1,0:T(8,128)S(1)} collective-permute-done((f32[256,256]{1,0:T(8,128)S(1)}, f32[256,256]{1,0:T(8,128)S(1)}, u32[]{:S(2)}, u32[]{:S(2)}) %collective-permute-start) | collective-permute-done | bytes 262176 | tf_op jit(solution)/shard_map/ppermute | solution.py:287
  78.7 9.8 %shard_map.19 = f32[4,56,128]{2,1,0:T(8,128)S(1)} custom-call(f32[256,256]{1,0:T(8,128)S(1)} %get-tuple-element.11.t_ref, f32[256,256]{1,0:T(8,128)S(1)} %collective-permute-done.b_ref), custom_call_target="tpu_custom_call" | custom-call | tf_op jit(solution)/shard_map/pallas_call | solution.py:259
  88.5 8.1 %all_to_all.22 = f32[4,56,128]{2,1,0:T(8,128)S(1)} all-to-all(f32[4,56,128]{2,1,0:T(8,128)S(1)} %shard_map.19), channel_id=1, replica_groups=mesh['grp'=16,'far'=4,'near'=4,'side'=2] {'near'}, dimensions={0} | all-to-all | bytes 229376 | tf_op jit(solution)/shard_map/all_to_all | solution.py:274
  96.7 21.9 %all_to_all.23.parts_ref = f32[8,56,128]{2,1,0:T(8,128)S(1)} all-to-all(f32[8,56,128]{2,1,0:T(8,128)S(1)} %broadcast_in_dim.19), channel_id=1, replica_groups=mesh['grp'=16,'far'=4,'near'=4,'side'=2] {'far','side'}, dimensions={0} | all-to-all | bytes 458752 | tf_op jit(solution)/shard_map/all_to_all | solution.py:279
  118.5 14.9 %shard_map.20 = f32[256,512]{1,0:T(8,128)} custom-call(f32[8,56,128]{2,1,0:T(8,128)S(1)} %all_to_all.23.parts_ref, f32[256,256]{1,0:T(8,128)S(1)} %get-tuple-element.11.t_ref, f32[256,256]{1,0:T(8,128)S(1)} %collective-permute-done.b_ref), custom_call_target="tpu_custom_call" | custom-call | tf_op jit(solution)/shard_map/pallas_call | solution.py:259
  (4 shorter events, 0.1 us)
Async XLA Ops:
  0.0 1.0 copy-start
  68.8 9.8 %collective-permute-start = (f32[256,256]{1,0:T(8,128)S(1)}, f32[256,256]{1,0:T(8,128)S(1)}, u32[]{:S(2)}, u32[]{:S(2)}) collective-permute-start(f32[256,256]{1,0:T(8,128)S(1)} %get-tuple-element.12), channel_id=1, source_target_pairs={{0,32},{32,64},{64,96},{96,128},{128,160},{160,192},{192,224},{224... | collective-permute-start | bytes 786440 | tf_op jit(solution)/shard_map/ppermute | solution.py:287
where the time goes:
time: 134 us; the launch traced here: 133 us
  blocking collectives  73.8 us (55%)
  Pallas kernels  48.7 us (36%)
  waiting for transfers between devices  7.87 us (6%)
  starting transfers between devices  1.94 us (1%)
    all_to_all x2, blocking collectives, exchanged(): return lax.all_to_all(again, FAR, 0, 0, tiled=True)  52.7 us
    pallas_call x4, Pallas kernels, call(): pl.pallas_call(body, out_shape=shapes, in_specs=[vmem] * len(args), out_s...  48.7 us
    all_to_all x2, blocking collectives, exchanged(): arrived = lax.all_to_all(parts, NEAR, 0, 0, tiled=True)  21 us
    ppermute x1, waiting for transfers between devices, per_device(): b = lax.ppermute(b, 'grp', [(i, (i + 1) % groups) for i in range(groups)])  7.87 us
  transfers between devices with their start and end apart: 1, of which 1 were waited for; matrix products, arithmetic and copies ran while one was open for 0% of the time, Pallas kernels for 0%

commit v1 on v0

v1 whole, which is shorter than its diff:
```python
import functools

import jax
import jax.numpy as jnp
from jax import lax
from jax.experimental import pallas as pl
from jax.experimental.pallas import tpu as pltpu
from jax.sharding import Mesh
from jax.sharding import PartitionSpec as P

ROUNDS = 6
HALF = 256
REACH = 10
EDGE = 32
DIAGS = 24
MID = 12
LINES = 56

f32 = jnp.float32
INTERPRET = False


def lanes(shape):
    return lax.broadcasted_iota(jnp.int32, shape, 1)


def turn_lanes(x, by):
    by %= x.shape[1]
    return pltpu.roll(x, by, axis=1) if by else x


def turn_lines(x, by):
    return pltpu.roll(x, by % x.shape[0], axis=0)


def picked(x, index):
    return jnp.take_along_axis(x, index, axis=1, mode="promise_in_bounds")


def mirrored(low, high):
    index = 127 - lanes(low.shape)
    return picked(high, index), picked(low, index)


def ends(t, b):
    at = lanes(t[0].shape)
    return jnp.where(
        at < 32, t[0], jnp.where(at < 64, turn_lanes(t[1], 64), jnp.where(at < 96, turn_lanes(b[0], 64), b[1]))
    )


def ahead(x, d):
    low, high = (turn_lanes(half, -d) for half in x)
    return jnp.where(lanes(low.shape) < 128 - d, low, high), high


def halves(ref, at):
    return ref[at, :128], ref[at, 128:256]


def band_of(load, count, out_ref, sums_ref):
    def over_rows(step, n, width):
        zeros = tuple(jnp.zeros((8, 128), f32) for _ in range(n * width))
        return lax.fori_loop(0, count, lambda k, sums: step(*load(k), sums), zeros, unroll=4)

    def with_top(t, b, sums):
        new = []
        for d in range(0, REACH + 1, 2):
            shifted = ahead(t, d) if d else t
            for left in (t, b) if d else (t,):
                new += [left[h] * shifted[h] for h in range(2)]
        return tuple(x + y for x, y in zip(sums, new))

    def with_bottom(t, b, sums):
        new = []
        for d in range(0, REACH + 1, 2):
            shifted = ahead(b, d) if d else b
            for left in (b, t):
                new += [left[h] * shifted[h] for h in range(2)]
        return tuple(x + y for x, y in zip(sums, new))

    def at_ends(t, b, sums):
        e = ends(t, b)
        swapped = turn_lanes(e, 64)
        new = [e * turn_lanes(e, -d) for d in range(1, REACH, 2)]
        new += [e * turn_lanes(swapped, -d) for d in range(1, REACH, 2)]
        return tuple(x + y for x, y in zip(sums, new))

    def keep(line, value):
        sums_ref[pl.ds(8 * line, 8), :] = value

    sums = over_rows(with_top, 11, 2)
    for h in range(2):
        keep(24 * h, sums[h])
        for j in range(1, 6):
            keep(24 * h + j, sums[4 * j - 2 + h])
            keep(24 * h + 17 + j, sums[4 * j + h])
    sums = over_rows(with_bottom, 12, 2)
    for h in range(2):
        for j in range(6):
            keep(24 * h + 6 + j, sums[4 * j + h])
            keep(24 * h + 12 + j, sums[4 * j + 2 + h])
    sums = over_rows(at_ends, 10, 1)
    for line, j in enumerate((0, 1, 2, 3, 5, 6, 7, 8)):
        keep(48 + line, sums[j])
    keep(23, sums[4])
    keep(47, sums[9])
    parts = [sums_ref[pl.ds(k, LINES, stride=8), :] for k in range(8)]
    while len(parts) > 1:
        parts = [x + y for x, y in zip(parts[::2], parts[1::2])]
    for k in range(out_ref.shape[0]):
        out_ref[k] = parts[0]


def spread(e, top):
    both = jnp.concatenate([e, e], axis=1)
    at = lanes(both.shape)
    first, last = (both, turn_lanes(both, 64)) if top else (turn_lanes(both, -64), both)
    return jnp.where(at < EDGE, first, jnp.where(at >= HALF - EDGE, last, 0.0))


def along_columns(x):
    shifted = jnp.broadcast_to(turn_lanes(x, -MID), (DIAGS, HALF))
    return pltpu.roll(shifted, 0, axis=1, stride=1, stride_axis=0)


def angles_of(parts_ref, x_ref):
    band = parts_ref[0]
    for k in range(1, parts_ref.shape[0]):
        band = band + parts_ref[k]
    low, high, narrow = band[:24], band[24:48], band[48:56]
    blank = jnp.zeros((1, HALF), f32)
    for block in range(4):
        for line in (0, DIAGS - 2, DIAGS - 1):
            x_ref[block, line : line + 1, :] = blank
    TT, TB, BT, BB = 0, 1, 2, 3

    def put(block, other, d, value):
        x_ref[block, MID - d : MID - d + 1, :] = value
        x_ref[other, MID + d : MID + d + 1, :] = turn_lanes(value, d)

    def line(k):
        return jnp.concatenate([low[k : k + 1], high[k : k + 1]], axis=1)

    for j in range(6):
        put(TT, TT, 2 * j, line(j))
        put(BB, BB, 2 * j, line(6 + j))
        put(TB, BT, 2 * j, line(12 + j))
        if j:
            put(BT, TB, 2 * j, line(17 + j))
    alike = jnp.concatenate([narrow[:4], low[23:24]], axis=0)
    across = jnp.concatenate([narrow[4:], high[23:24]], axis=0)
    odd = [
        (TT, TT, spread(alike, True)),
        (BB, BB, spread(alike, False)),
        (TB, BT, spread(across, True)),
        (BT, TB, spread(across, False)),
    ]
    for block, other, value in odd:
        for j in range(5):
            put(block, other, 2 * j + 1, value[j : j + 1])

    tt, tb, bt, bb = (x_ref[k] for k in range(4))
    shape = (DIAGS, HALF)
    i = lanes(shape)
    j = i + MID - lax.broadcasted_iota(jnp.int32, shape, 0)
    i_one, i_more, i_last = i == 1, i >= 2, i == HALF - 1
    j_one, j_more, j_last = j == 1, j >= 2, j == HALF - 1

    def less(x):
        return turn_lines(x, -1)

    def more(x):
        return turn_lines(x, 1)

    cosines, sines = [], []
    for turn in range(ROUNDS):
        first, second, coupling = (x[MID : MID + 1] for x in (tt, bb, tb))
        difference = second - first
        direction = jnp.where(difference >= 0, 1.0, -1.0)
        denominator = (
            jnp.abs(difference)
            + jnp.sqrt(difference * difference + 4.0 * coupling * coupling)
            + 1e-06 * (first + second)
        )
        tangent = direction * 2.0 * coupling / denominator
        c = 1.0 / jnp.sqrt(1.0 + tangent * tangent)
        s = tangent * c
        cosines.append(c)
        sines.append(s)
        if turn == ROUNDS - 1:
            break
        c_row, s_row = jnp.broadcast_to(c, shape), jnp.broadcast_to(s, shape)
        c_col, s_col = along_columns(c), along_columns(s)
        tt, tb = c_col * tt - s_col * tb, s_col * tt + c_col * tb
        bt, bb = c_col * bt - s_col * bb, s_col * bt + c_col * bb
        tt, bt = c_row * tt - s_row * bt, s_row * tt + c_row * bt
        tb, bb = c_row * tb - s_row * bb, s_row * tb + c_row * bb
        tt, tb = (
            jnp.where(j_more, less(tt), jnp.where(j_one, less(tb), tt)),
            jnp.where(j_last, tt, more(tb)),
        )
        bt, bb = (
            jnp.where(j_more, less(bt), jnp.where(j_one, less(bb), bt)),
            jnp.where(j_last, bt, more(bb)),
        )
        tt, bt = (
            jnp.where(i_more, turn_lanes(more(tt), 1), jnp.where(i_one, turn_lanes(more(bt), 1), tt)),
            jnp.where(i_last, tt, turn_lanes(less(bt), -1)),
        )
        tb, bb = (
            jnp.where(i_more, turn_lanes(more(tb), 1), jnp.where(i_one, turn_lanes(more(bb), 1), tb)),
            jnp.where(i_last, tb, turn_lanes(less(bb), -1)),
        )
    return cosines, sines


def advanced(t, b):
    at = lanes(t[0].shape)
    t0, t1, b0, b1 = turn_lanes(t[0], 1), turn_lanes(t[1], 1), turn_lanes(b[0], -1), turn_lanes(b[1], -1)
    return (
        (
            jnp.where(at >= 2, t0, jnp.where(at == 1, turn_lanes(b[0], 1), t[0])),
            jnp.where(at >= 1, t1, t0),
        ),
        (jnp.where(at == 127, b1, b0), jnp.where(at == 127, t[1], b1)),
    )


MOVES = ROUNDS - 1


def retreated_top(t, b):
    at = lanes(t[0].shape)
    back = [turn_lanes(x, -MOVES) for x in t]
    from_bottom = picked(b[1], (250 - at) % 128)
    return (
        jnp.where(at == 0, t[0], jnp.where(at < 128 - MOVES, back[0], back[1])),
        jnp.where(at < 128 - MOVES, back[1], from_bottom),
    )


def retreated_bottom(t, b):
    at = lanes(t[0].shape)
    on = [turn_lanes(x, MOVES) for x in b]
    from_top = picked(t[0], (MOVES - at) % 128)
    return (
        jnp.where(at < MOVES, from_top, on[0]),
        jnp.where(at < MOVES, on[0], on[1]),
    )


def unfolded_bottom(t, b):
    at = lanes(t[0].shape)
    index = (122 - at) % 128
    low, high = picked(b[0], index), picked(b[1], index)
    return (
        jnp.where(at <= 122, high, low),
        jnp.where(at <= 122, low, turn_lanes(t[0], 122)),
    )


def turned_chunks(load, store, count, rows, cosines, sines):
    def chunk(k, carry):
        t, b = load(k)
        for turn in range(ROUNDS):
            c, s = cosines[turn], sines[turn]
            t, b = (
                tuple(c[h] * t[h] - s[h] * b[h] for h in range(2)),
                tuple(s[h] * t[h] + c[h] * b[h] for h in range(2)),
            )
            if turn < MOVES:
                t, b = advanced(t, b)
        store(k, t, b)
        return carry

    def wide(x):
        x = jnp.broadcast_to(x, (rows, HALF))
        return x[:, :128], x[:, 128:]

    cosines, sines = [wide(c) for c in cosines], [wide(s) for s in sines]
    lax.fori_loop(0, count, chunk, 0)


def rows_at(k, rows):
    return pl.ds(pl.multiple_of(k * rows, rows), rows)


CHUNK = 32


def first_band(p_ref, out_ref, b_ref, sums_ref):
    def fold(k, carry):
        at = rows_at(k, CHUNK)
        b_ref[at, :128], b_ref[at, 128:] = mirrored(p_ref[at, 256:384], p_ref[at, 384:])
        return carry

    lax.fori_loop(0, p_ref.shape[0] // CHUNK, fold, 0)

    def load(k):
        at = rows_at(k, 8)
        return halves(p_ref, at), halves(b_ref, at)

    band_of(load, p_ref.shape[0] // 8, out_ref, sums_ref)


def second_band(t_ref, b_ref, out_ref, sums_ref):
    def load(k):
        at = rows_at(k, 8)
        return halves(t_ref, at), halves(b_ref, at)

    band_of(load, t_ref.shape[0] // 8, out_ref, sums_ref)


def first_turn(parts_ref, t_ref, b_ref, t_out, b_out, x_ref):
    cosines, sines = angles_of(parts_ref, x_ref)

    def load(k):
        at = rows_at(k, CHUNK)
        return halves(t_ref, at), halves(b_ref, at)

    def store(k, t, b):
        at = rows_at(k, CHUNK)
        t_out[at, :128], t_out[at, 128:] = retreated_top(t, b)
        b_out[at, :128], b_out[at, 128:] = retreated_bottom(t, b)

    turned_chunks(load, store, t_ref.shape[0] // CHUNK, CHUNK, cosines, sines)


def second_turn(parts_ref, t_ref, b_ref, out_ref, x_ref):
    cosines, sines = angles_of(parts_ref, x_ref)

    def load(k):
        at = rows_at(k, CHUNK)
        return halves(t_ref, at), halves(b_ref, at)

    def store(k, t, b):
        at = rows_at(k, CHUNK)
        out_ref[at, :128], out_ref[at, 128:256] = retreated_top(t, b)
        out_ref[at, 256:384], out_ref[at, 384:] = unfolded_bottom(t, b)

    turned_chunks(load, store, t_ref.shape[0] // CHUNK, CHUNK, cosines, sines)


def call(body, outs, args, scratch=()):
    vmem = pl.BlockSpec(memory_space=pltpu.VMEM)
    shapes = [jax.ShapeDtypeStruct(s, f32) for s in outs]
    return pl.pallas_call(
        body,
        out_shape=shapes,
        in_specs=[vmem] * len(args),
        out_specs=[vmem] * len(outs),
        scratch_shapes=[pltpu.VMEM(s, f32) for s in scratch],
        compiler_params=pltpu.CompilerParams(vmem_limit_bytes=32 * 1024 * 1024),
        interpret=INTERPRET,
    )(*args)


NEAR, FAR = ("near",), ("far", "side")


def exchanged(parts, near, far):
    arrived = lax.all_to_all(parts, NEAR, 0, 0, tiled=True)
    total = arrived[0]
    for k in range(1, near):
        total = total + arrived[k]
    again = jnp.broadcast_to(total[None], (far, *total.shape))
    return lax.all_to_all(again, FAR, 0, 0, tiled=True)


SUMS = [(8 * LINES, 128)]
STATE = [(4, DIAGS, HALF)]


def per_device(snapshots, near, far, groups):
    rows = snapshots.shape[0]
    square, band = (rows, HALF), (near, LINES, 128)
    parts, b = call(first_band, [band, square], [snapshots], SUMS)
    t, b = call(first_turn, [square, square], [exchanged(parts, near, far), snapshots, b], STATE)
    b = lax.ppermute(b, "grp", [(i, (i + 1) % groups) for i in range(groups)])
    (parts,) = call(second_band, [band], [t, b], SUMS)
    (out,) = call(second_turn, [(rows, 2 * HALF)], [exchanged(parts, near, far), t, b], STATE)
    return out


def solution(mesh):
    groups, rows = mesh.shape["grp"], mesh.shape["row"]
    near, side = 4, 2
    far = rows // (near * side)
    fine = Mesh(mesh.devices.reshape(groups, far, near, side), ("grp", "far", "near", "side"))
    placed = P(("far", "near", "side"), "grp")
    body = functools.partial(per_device, near=near, far=far * side, groups=groups)
    return jax.shard_map(body, mesh=fine, in_specs=(placed,), out_specs=placed, check_vma=False)
```

time: 134 us -> 106 us (0.79)
  Pallas kernels: 48.7 us -> 20.6 us
    pallas_call x4, Pallas kernels: 48.7 us -> 20.6 us  [call(): pl.pallas_call(body, out_shape=shapes, in_specs=[vmem] * len(args), out_s...]
where the time goes in v1:
time: 106 us; the launch traced here: 105 us
  blocking collectives  73.8 us (70%)
  Pallas kernels  20.6 us (19%)
  waiting for transfers between devices  7.87 us (7%)
  starting transfers between devices  1.92 us (2%)
  local copies, waits for them, and re-layouts  1.07 us (1%)
    all_to_all x2, blocking collectives, exchanged(): return lax.all_to_all(again, FAR, 0, 0, tiled=True)  52.8 us
    all_to_all x2, blocking collectives, exchanged(): arrived = lax.all_to_all(parts, NEAR, 0, 0, tiled=True)  21 us
    pallas_call x4, Pallas kernels, call(): pl.pallas_call(body, out_shape=shapes, in_specs=[vmem] * len(args), out_s...  20.6 us
    ppermute x1, waiting for transfers between devices, per_device(): b = lax.ppermute(b, 'grp', [(i, (i + 1) % groups) for i in range(groups)])  7.87 us
  transfers between devices with their start and end apart: 1, of which 1 were waited for; matrix products, arithmetic and copies ran while one was open for 0% of the time, Pallas kernels for 0%

profile of v1, /device:TPU:32, one launch (start us, length us, event | category | flops | bytes accessed | tf_op | source)
XLA Modules:
  0.0 105.3 jit_solution(9733447020425126669)
XLA Ops:
  0.0 0.0 copy-start
  0.0 1.0 copy-done
  1.0 4.3 %shard_map.17 = (f32[4,56,128]{2,1,0:T(8,128)S(1)}, f32[256,256]{1,0:T(8,128)S(1)}) custom-call(f32[256,512]{1,0:T(8,128)S(1)} %copy-done), custom_call_target="tpu_custom_call" | custom-call | tf_op jit(solution)/shard_map/pallas_call | solution.py:348
  5.4 12.9 %all_to_all.20 = f32[4,56,128]{2,1,0:T(8,128)S(1)} all-to-all(f32[4,56,128]{2,1,0:T(8,128)S(1)} %get-tuple-element.9), channel_id=1, replica_groups=mesh['grp'=16,'far'=4,'near'=4,'side'=2] {'near'}, dimensions={0} | all-to-all | bytes 229376 | tf_op jit(solution)/shard_map/all_to_all | solution.py:363
  18.3 30.9 %all_to_all.21.parts_ref = f32[8,56,128]{2,1,0:T(8,128)S(1)} all-to-all(f32[8,56,128]{2,1,0:T(8,128)S(1)} %broadcast_in_dim.17), channel_id=1, replica_groups=mesh['grp'=16,'far'=4,'near'=4,'side'=2] {'far','side'}, dimensions={0} | all-to-all | bytes 458752 | tf_op jit(solution)/shard_map/all_to_all | solution.py:368
  49.2 5.9 %shard_map.18 = (f32[256,256]{1,0:T(8,128)S(1)}, f32[256,256]{1,0:T(8,128)S(1)}) custom-call(f32[8,56,128]{2,1,0:T(8,128)S(1)} %all_to_all.21.parts_ref, f32[256,512]{1,0:T(8,128)S(1)} %copy-done, f32[256,256]{1,0:T(8,128)S(1)} %get-tuple-element.10.b_ref), custom_call_target="tpu_custom_call" | custom-call | tf_op jit(solution)/shard_map/pallas_call | solution.py:348
  55.1 1.9 %collective-permute-start = (f32[256,256]{1,0:T(8,128)S(1)}, f32[256,256]{1,0:T(8,128)S(1)}, u32[]{:S(2)}, u32[]{:S(2)}) collective-permute-start(f32[256,256]{1,0:T(8,128)S(1)} %get-tuple-element.12), channel_id=1, source_target_pairs={{0,32},{32,64},{64,96},{96,128},{128,160},{160,192},{192,224},{224... | collective-permute-start | bytes 786440 | tf_op jit(solution)/shard_map/ppermute | solution.py:380
  57.0 7.9 %collective-permute-done.b_ref = f32[256,256]{1,0:T(8,128)S(1)} collective-permute-done((f32[256,256]{1,0:T(8,128)S(1)}, f32[256,256]{1,0:T(8,128)S(1)}, u32[]{:S(2)}, u32[]{:S(2)}) %collective-permute-start) | collective-permute-done | bytes 262176 | tf_op jit(solution)/shard_map/ppermute | solution.py:380
  64.9 3.7 %shard_map.19 = f32[4,56,128]{2,1,0:T(8,128)S(1)} custom-call(f32[256,256]{1,0:T(8,128)S(1)} %get-tuple-element.11.t_ref, f32[256,256]{1,0:T(8,128)S(1)} %collective-permute-done.b_ref), custom_call_target="tpu_custom_call" | custom-call | tf_op jit(solution)/shard_map/pallas_call | solution.py:348
  68.6 8.1 %all_to_all.22 = f32[4,56,128]{2,1,0:T(8,128)S(1)} all-to-all(f32[4,56,128]{2,1,0:T(8,128)S(1)} %shard_map.19), channel_id=1, replica_groups=mesh['grp'=16,'far'=4,'near'=4,'side'=2] {'near'}, dimensions={0} | all-to-all | bytes 229376 | tf_op jit(solution)/shard_map/all_to_all | solution.py:363
  76.8 21.9 %all_to_all.23.parts_ref = f32[8,56,128]{2,1,0:T(8,128)S(1)} all-to-all(f32[8,56,128]{2,1,0:T(8,128)S(1)} %broadcast_in_dim.19), channel_id=1, replica_groups=mesh['grp'=16,'far'=4,'near'=4,'side'=2] {'far','side'}, dimensions={0} | all-to-all | bytes 458752 | tf_op jit(solution)/shard_map/all_to_all | solution.py:368
  98.6 6.7 %shard_map.20 = f32[256,512]{1,0:T(8,128)} custom-call(f32[8,56,128]{2,1,0:T(8,128)S(1)} %all_to_all.23.parts_ref, f32[256,256]{1,0:T(8,128)S(1)} %get-tuple-element.11.t_ref, f32[256,256]{1,0:T(8,128)S(1)} %collective-permute-done.b_ref), custom_call_target="tpu_custom_call" | custom-call | tf_op jit(solution)/shard_map/pallas_call | solution.py:348
  (4 shorter events, 0.1 us)
Async XLA Ops:
  0.0 1.0 copy-start
  55.1 9.8 %collective-permute-start = (f32[256,256]{1,0:T(8,128)S(1)}, f32[256,256]{1,0:T(8,128)S(1)}, u32[]{:S(2)}, u32[]{:S(2)}) collective-permute-start(f32[256,256]{1,0:T(8,128)S(1)} %get-tuple-element.12), channel_id=1, source_target_pairs={{0,32},{32,64},{64,96},{96,128},{128,160},{160,192},{192,224},{224... | collective-permute-start | bytes 786440 | tf_op jit(solution)/shard_map/ppermute | solution.py:380

commit v2 on v1

--- a/solution.py
+++ b/solution.py
@@ -61,7 +61,7 @@
 def band_of(load, count, out_ref, sums_ref):
     def over_rows(step, n, width):
         zeros = tuple(jnp.zeros((8, 128), f32) for _ in range(n * width))
-        return lax.fori_loop(0, count, lambda k, sums: step(*load(k), sums), zeros, unroll=4)
+        return lax.fori_loop(0, count, lambda k, sums: step(*load(k), sums), zeros, unroll=16)
 
     def with_top(t, b, sums):
         new = []
@@ -286,7 +286,7 @@
     return pl.ds(pl.multiple_of(k * rows, rows), rows)
 
 
-CHUNK = 32
+CHUNK = 256
 
 
 def first_band(p_ref, out_ref, b_ref, sums_ref):

time: 106 us -> 95.3 us (0.90)
  Pallas kernels: 20.6 us -> 10.3 us
    pallas_call x4, Pallas kernels: 20.6 us -> 10.3 us  [call(): pl.pallas_call(body, out_shape=shapes, in_specs=[vmem] * len(args), out_s...]
where the time goes in v2:
time: 95.3 us; the launch traced here: 95 us
  blocking collectives  73.8 us (77%)
  Pallas kernels  10.3 us (11%)
  waiting for transfers between devices  7.87 us (8%)
  starting transfers between devices  1.92 us (2%)
  local copies, waits for them, and re-layouts  1.07 us (1%)
    all_to_all x2, blocking collectives, exchanged(): return lax.all_to_all(again, FAR, 0, 0, tiled=True)  52.8 us
    all_to_all x2, blocking collectives, exchanged(): arrived = lax.all_to_all(parts, NEAR, 0, 0, tiled=True)  21 us
    pallas_call x4, Pallas kernels, call(): pl.pallas_call(body, out_shape=shapes, in_specs=[vmem] * len(args), out_s...  10.3 us
    ppermute x1, waiting for transfers between devices, per_device(): b = lax.ppermute(b, 'grp', [(i, (i + 1) % groups) for i in range(groups)])  7.87 us
    ppermute x1, starting transfers between devices, per_device(): b = lax.ppermute(b, 'grp', [(i, (i + 1) % groups) for i in range(groups)])  1.92 us
  transfers between devices with their start and end apart: 1, of which 1 were waited for; matrix products, arithmetic and copies ran while one was open for 0% of the time, Pallas kernels for 0%

profile of v2, /device:TPU:32, one launch (start us, length us, event | category | flops | bytes accessed | tf_op | source)
XLA Modules:
  0.0 95.0 jit_solution(13441675267904968376)
XLA Ops:
  0.0 0.0 copy-start
  0.0 1.0 %copy-done = f32[256,512]{1,0:T(8,128)S(1)} copy-done((f32[256,512]{1,0:T(8,128)S(1)}, f32[256,512]{1,0:T(8,128)}, u32[]{:S(2)}) %copy-start) | copy-done | bytes 524312
  1.0 1.9 %shard_map.17 = (f32[4,56,128]{2,1,0:T(8,128)S(1)}, f32[256,256]{1,0:T(8,128)S(1)}) custom-call(f32[256,512]{1,0:T(8,128)S(1)} %copy-done), custom_call_target="tpu_custom_call" | custom-call | tf_op jit(solution)/shard_map/pallas_call | solution.py:348
  3.0 12.9 %all_to_all.20 = f32[4,56,128]{2,1,0:T(8,128)S(1)} all-to-all(f32[4,56,128]{2,1,0:T(8,128)S(1)} %get-tuple-element.9), channel_id=1, replica_groups=mesh['grp'=16,'far'=4,'near'=4,'side'=2] {'near'}, dimensions={0} | all-to-all | bytes 229376 | tf_op jit(solution)/shard_map/all_to_all | solution.py:363
  15.9 30.9 %all_to_all.21.parts_ref = f32[8,56,128]{2,1,0:T(8,128)S(1)} all-to-all(f32[8,56,128]{2,1,0:T(8,128)S(1)} %broadcast_in_dim.17), channel_id=1, replica_groups=mesh['grp'=16,'far'=4,'near'=4,'side'=2] {'far','side'}, dimensions={0} | all-to-all | bytes 458752 | tf_op jit(solution)/shard_map/all_to_all | solution.py:368
  46.8 2.9 %shard_map.18 = (f32[256,256]{1,0:T(8,128)S(1)}, f32[256,256]{1,0:T(8,128)S(1)}) custom-call(f32[8,56,128]{2,1,0:T(8,128)S(1)} %all_to_all.21.parts_ref, f32[256,512]{1,0:T(8,128)S(1)} %copy-done, f32[256,256]{1,0:T(8,128)S(1)} %get-tuple-element.10.b_ref), custom_call_target="tpu_custom_call" | custom-call | tf_op jit(solution)/shard_map/pallas_call | solution.py:348
  49.7 1.9 %collective-permute-start = (f32[256,256]{1,0:T(8,128)S(1)}, f32[256,256]{1,0:T(8,128)S(1)}, u32[]{:S(2)}, u32[]{:S(2)}) collective-permute-start(f32[256,256]{1,0:T(8,128)S(1)} %get-tuple-element.12), channel_id=1, source_target_pairs={{0,32},{32,64},{64,96},{96,128},{128,160},{160,192},{192,224},{224... | collective-permute-start | bytes 786440 | tf_op jit(solution)/shard_map/ppermute | solution.py:380
  51.6 7.9 %collective-permute-done.b_ref = f32[256,256]{1,0:T(8,128)S(1)} collective-permute-done((f32[256,256]{1,0:T(8,128)S(1)}, f32[256,256]{1,0:T(8,128)S(1)}, u32[]{:S(2)}, u32[]{:S(2)}) %collective-permute-start) | collective-permute-done | bytes 262176 | tf_op jit(solution)/shard_map/ppermute | solution.py:380
  59.5 1.8 %shard_map.19 = f32[4,56,128]{2,1,0:T(8,128)S(1)} custom-call(f32[256,256]{1,0:T(8,128)S(1)} %get-tuple-element.11.t_ref, f32[256,256]{1,0:T(8,128)S(1)} %collective-permute-done.b_ref), custom_call_target="tpu_custom_call" | custom-call | tf_op jit(solution)/shard_map/pallas_call | solution.py:348
  61.3 8.1 %all_to_all.22 = f32[4,56,128]{2,1,0:T(8,128)S(1)} all-to-all(f32[4,56,128]{2,1,0:T(8,128)S(1)} %shard_map.19), channel_id=1, replica_groups=mesh['grp'=16,'far'=4,'near'=4,'side'=2] {'near'}, dimensions={0} | all-to-all | bytes 229376 | tf_op jit(solution)/shard_map/all_to_all | solution.py:363
  69.5 21.9 %all_to_all.23.parts_ref = f32[8,56,128]{2,1,0:T(8,128)S(1)} all-to-all(f32[8,56,128]{2,1,0:T(8,128)S(1)} %broadcast_in_dim.19), channel_id=1, replica_groups=mesh['grp'=16,'far'=4,'near'=4,'side'=2] {'far','side'}, dimensions={0} | all-to-all | bytes 458752 | tf_op jit(solution)/shard_map/all_to_all | solution.py:368
  91.3 3.6 %shard_map.20 = f32[256,512]{1,0:T(8,128)} custom-call(f32[8,56,128]{2,1,0:T(8,128)S(1)} %all_to_all.23.parts_ref, f32[256,256]{1,0:T(8,128)S(1)} %get-tuple-element.11.t_ref, f32[256,256]{1,0:T(8,128)S(1)} %collective-permute-done.b_ref), custom_call_target="tpu_custom_call" | custom-call | tf_op jit(solution)/shard_map/pallas_call | solution.py:348
  (4 shorter events, 0.1 us)
Async XLA Ops:
  0.0 1.0 %copy-start = (f32[256,512]{1,0:T(8,128)S(1)}, f32[256,512]{1,0:T(8,128)}, u32[]{:S(2)}) copy-start(f32[256,512]{1,0:T(8,128)} %t_ref.1) | copy-start | bytes 1572868
  49.7 9.8 %collective-permute-start = (f32[256,256]{1,0:T(8,128)S(1)}, f32[256,256]{1,0:T(8,128)S(1)}, u32[]{:S(2)}, u32[]{:S(2)}) collective-permute-start(f32[256,256]{1,0:T(8,128)S(1)} %get-tuple-element.12), channel_id=1, source_target_pairs={{0,32},{32,64},{64,96},{96,128},{128,160},{160,192},{192,224},{224... | collective-permute-start | bytes 786440 | tf_op jit(solution)/shard_map/ppermute | solution.py:380

commit v3 on v2

--- a/solution.py
+++ b/solution.py
@@ -11,10 +11,11 @@
 ROUNDS = 6
 HALF = 256
 REACH = 10
-EDGE = 32
 DIAGS = 24
 MID = 12
-LINES = 56
+WIDE = 23
+LINES = 48
+WINDOW = 16
 
 f32 = jnp.float32
 INTERPRET = False
@@ -44,9 +45,41 @@
 
 def ends(t, b):
     at = lanes(t[0].shape)
-    return jnp.where(
-        at < 32, t[0], jnp.where(at < 64, turn_lanes(t[1], 64), jnp.where(at < 96, turn_lanes(b[0], 64), b[1]))
+    e = jnp.where(
+        at < 16,
+        t[0],
+        jnp.where(at < 32, turn_lanes(t[1], 26), jnp.where(at < 48, turn_lanes(b[0], 32), turn_lanes(b[1], 58))),
     )
+    swapped = jnp.where(at < 96, turn_lanes(e, 32), turn_lanes(e, 96))
+    return jnp.where(at < 64, e, turn_lanes(e, 64)), jnp.where(at < 64, e, swapped)
+
+
+def place_of_odd(shape):
+    k = lax.broadcasted_iota(jnp.int32, shape, 0)
+    return k, REACH // 2 - k, (k * (REACH + 1 - k)) // 2
+
+
+def packed_odd(sums):
+    k, count, start = place_of_odd(sums.shape)
+    at = lanes(sums.shape)
+    inside = at % WINDOW - start
+    first = jnp.where((at // WINDOW) % 2 == 0, 0, REACH // 2 - 1 - k)
+    index = jnp.clip(at - at % WINDOW + first + inside, 0, 127)
+    used = (k < REACH // 2) & (inside >= 0) & (inside < count)
+    return jnp.sum(jnp.where(used, picked(sums, index), 0.0), axis=0, keepdims=True)
+
+
+def unpacked_odd(line, window, mirror):
+    line = jnp.broadcast_to(line, (8, 128))
+    k, count, start = place_of_odd(line.shape)
+    at = lanes(line.shape) - (2 * k + 1 if mirror else 0)
+    out = []
+    for end in range(2):
+        inside = at - (128 - REACH + REACH // 2 - 1 - k if end else 0)
+        used = (k < REACH // 2) & (inside >= 0) & (inside < count)
+        index = jnp.clip((window + end) * WINDOW + start + inside, 0, 127)
+        out.append(jnp.where(used, picked(line, index), 0.0))
+    return jnp.concatenate(out, axis=1)
 
 
 def ahead(x, d):
@@ -80,10 +113,8 @@
         return tuple(x + y for x, y in zip(sums, new))
 
     def at_ends(t, b, sums):
-        e = ends(t, b)
-        swapped = turn_lanes(e, 64)
-        new = [e * turn_lanes(e, -d) for d in range(1, REACH, 2)]
-        new += [e * turn_lanes(swapped, -d) for d in range(1, REACH, 2)]
+        left, right = ends(t, b)
+        new = [left * turn_lanes(right, -d) for d in range(1, REACH, 2)]
         return tuple(x + y for x, y in zip(sums, new))
 
     def keep(line, value):
@@ -100,23 +131,18 @@
         for j in range(6):
             keep(24 * h + 6 + j, sums[4 * j + h])
             keep(24 * h + 12 + j, sums[4 * j + 2 + h])
-    sums = over_rows(at_ends, 10, 1)
-    for line, j in enumerate((0, 1, 2, 3, 5, 6, 7, 8)):
-        keep(48 + line, sums[j])
-    keep(23, sums[4])
-    keep(47, sums[9])
-    parts = [sums_ref[pl.ds(k, LINES, stride=8), :] for k in range(8)]
+    sums = over_rows(at_ends, 5, 1)
+    for j in range(5):
+        keep(LINES + j, sums[j])
+    for line in (WIDE, LINES - 1, LINES + 5, LINES + 6, LINES + 7):
+        keep(line, jnp.zeros((8, 128), f32))
+    parts = [sums_ref[pl.ds(k, LINES + 8, stride=8), :] for k in range(8)]
     while len(parts) > 1:
         parts = [x + y for x, y in zip(parts[::2], parts[1::2])]
+    odd = packed_odd(parts[0][LINES:])
     for k in range(out_ref.shape[0]):
-        out_ref[k] = parts[0]
-
-
-def spread(e, top):
-    both = jnp.concatenate([e, e], axis=1)
-    at = lanes(both.shape)
-    first, last = (both, turn_lanes(both, 64)) if top else (turn_lanes(both, -64), both)
-    return jnp.where(at < EDGE, first, jnp.where(at >= HALF - EDGE, last, 0.0))
+        out_ref[k] = parts[0][:LINES]
+        out_ref[k, WIDE : WIDE + 1, :] = odd
 
 
 def along_columns(x):
@@ -128,7 +154,7 @@
     band = parts_ref[0]
     for k in range(1, parts_ref.shape[0]):
         band = band + parts_ref[k]
-    low, high, narrow = band[:24], band[24:48], band[48:56]
+    low, high = band[:24], band[24:]
     blank = jnp.zeros((1, HALF), f32)
     for block in range(4):
         for line in (0, DIAGS - 2, DIAGS - 1):
@@ -148,17 +174,13 @@
         put(TB, BT, 2 * j, line(12 + j))
         if j:
             put(BT, TB, 2 * j, line(17 + j))
-    alike = jnp.concatenate([narrow[:4], low[23:24]], axis=0)
-    across = jnp.concatenate([narrow[4:], high[23:24]], axis=0)
-    odd = [
-        (TT, TT, spread(alike, True)),
-        (BB, BB, spread(alike, False)),
-        (TB, BT, spread(across, True)),
-        (BT, TB, spread(across, False)),
-    ]
-    for block, other, value in odd:
+    for window, (block, other) in enumerate(((TT, TT), (BB, BB), (TB, BT), (BT, TB))):
+        there = unpacked_odd(low[WIDE : WIDE + 1], 2 * window, False)
+        mirror = unpacked_odd(low[WIDE : WIDE + 1], 2 * window, True)
         for j in range(5):
-            put(block, other, 2 * j + 1, value[j : j + 1])
+            d = 2 * j + 1
+            x_ref[block, MID - d : MID - d + 1, :] = there[j : j + 1]
+            x_ref[other, MID + d : MID + d + 1, :] = mirror[j : j + 1]
 
     tt, tb, bt, bb = (x_ref[k] for k in range(4))
     shape = (DIAGS, HALF)
@@ -356,7 +378,7 @@
     )(*args)
 
 
-NEAR, FAR = ("near",), ("far", "side")
+NEAR, FAR = "near", "far"
 
 
 def exchanged(parts, near, far):
@@ -368,7 +390,7 @@
     return lax.all_to_all(again, FAR, 0, 0, tiled=True)
 
 
-SUMS = [(8 * LINES, 128)]
+SUMS = [(8 * LINES + 64, 128)]
 STATE = [(4, DIAGS, HALF)]
 
 
@@ -385,9 +407,8 @@
 
 def solution(mesh):
     groups, rows = mesh.shape["grp"], mesh.shape["row"]
-    near, side = 4, 2
-    far = rows // (near * side)
-    fine = Mesh(mesh.devices.reshape(groups, far, near, side), ("grp", "far", "near", "side"))
-    placed = P(("far", "near", "side"), "grp")
-    body = functools.partial(per_device, near=near, far=far * side, groups=groups)
+    near, far = 4, rows // 4
+    fine = Mesh(mesh.devices.reshape(groups, far, near), ("grp", "far", "near"))
+    placed = P(("far", "near"), "grp")
+    body = functools.partial(per_device, near=near, far=far, groups=groups)
     return jax.shard_map(body, mesh=fine, in_specs=(placed,), out_specs=placed, check_vma=False)

time: 95.3 us -> 90.7 us (0.952)
  the two profiles are of different devices: /device:TPU:32 before, /device:TPU:8 now
where the time goes in v3:
time: 90.7 us; the launch traced here: 90.4 us
  blocking collectives  71.8 us (79%)
  Pallas kernels  9.75 us (11%)
  waiting for transfers between devices  5.76 us (6%)
  starting transfers between devices  1.92 us (2%)
  local copies, waits for them, and re-layouts  1.07 us (1%)
    all_to_all x2, blocking collectives, exchanged(): return lax.all_to_all(again, FAR, 0, 0, tiled=True)  51.2 us
    all_to_all x2, blocking collectives, exchanged(): arrived = lax.all_to_all(parts, NEAR, 0, 0, tiled=True)  20.7 us
    pallas_call x4, Pallas kernels, call(): pl.pallas_call(body, out_shape=shapes, in_specs=[vmem] * len(args), out_s...  9.75 us
    ppermute x1, waiting for transfers between devices, per_device(): b = lax.ppermute(b, 'grp', [(i, (i + 1) % groups) for i in range(groups)])  5.76 us
    ppermute x1, starting transfers between devices, per_device(): b = lax.ppermute(b, 'grp', [(i, (i + 1) % groups) for i in range(groups)])  1.92 us
  transfers between devices with their start and end apart: 1, of which 1 were waited for; matrix products, arithmetic and copies ran while one was open for 0% of the time, Pallas kernels for 0%

profile of v3, /device:TPU:8, one launch (start us, length us, event | category | flops | bytes accessed | tf_op | source)
XLA Modules:
  0.0 90.4 jit_solution(12859333402221430984)
XLA Ops:
  0.0 0.0 copy-start
  0.0 1.0 %copy-done = f32[256,512]{1,0:T(8,128)S(1)} copy-done((f32[256,512]{1,0:T(8,128)S(1)}, f32[256,512]{1,0:T(8,128)}, u32[]{:S(2)}) %copy-start) | copy-done | bytes 524312
  1.0 1.8 %shard_map.17 = (f32[4,48,128]{2,1,0:T(8,128)S(1)}, f32[256,256]{1,0:T(8,128)S(1)}) custom-call(f32[256,512]{1,0:T(8,128)S(1)} %copy-done), custom_call_target="tpu_custom_call" | custom-call | tf_op jit(solution)/shard_map/pallas_call | solution.py:370
  2.8 11.9 %all_to_all.20 = f32[4,48,128]{2,1,0:T(8,128)S(1)} all-to-all(f32[4,48,128]{2,1,0:T(8,128)S(1)} %get-tuple-element.9), channel_id=1, replica_groups=mesh['grp'=16,'far'=8,'near'=4] {'near'}, dimensions={0} | all-to-all | bytes 196608 | tf_op jit(solution)/shard_map/all_to_all | solution.py:385
  14.8 31.4 %all_to_all.21.parts_ref = f32[8,48,128]{2,1,0:T(8,128)S(1)} all-to-all(f32[8,48,128]{2,1,0:T(8,128)S(1)} %broadcast_in_dim.17), channel_id=1, replica_groups=mesh['grp'=16,'far'=8,'near'=4] {'far'}, dimensions={0} | all-to-all | bytes 393216 | tf_op jit(solution)/shard_map/all_to_all | solution.py:390
  46.2 2.7 %shard_map.18 = (f32[256,256]{1,0:T(8,128)S(1)}, f32[256,256]{1,0:T(8,128)S(1)}) custom-call(f32[8,48,128]{2,1,0:T(8,128)S(1)} %all_to_all.21.parts_ref, f32[256,512]{1,0:T(8,128)S(1)} %copy-done, f32[256,256]{1,0:T(8,128)S(1)} %get-tuple-element.10.b_ref), custom_call_target="tpu_custom_call" | custom-call | tf_op jit(solution)/shard_map/pallas_call | solution.py:370
  48.9 1.9 %collective-permute-start = (f32[256,256]{1,0:T(8,128)S(1)}, f32[256,256]{1,0:T(8,128)S(1)}, u32[]{:S(2)}, u32[]{:S(2)}) collective-permute-start(f32[256,256]{1,0:T(8,128)S(1)} %get-tuple-element.12), channel_id=1, source_target_pairs={{0,32},{32,64},{64,96},{96,128},{128,160},{160,192},{192,224},{224... | collective-permute-start | bytes 786440 | tf_op jit(solution)/shard_map/ppermute | solution.py:402
  50.8 5.8 %collective-permute-done.b_ref = f32[256,256]{1,0:T(8,128)S(1)} collective-permute-done((f32[256,256]{1,0:T(8,128)S(1)}, f32[256,256]{1,0:T(8,128)S(1)}, u32[]{:S(2)}, u32[]{:S(2)}) %collective-permute-start) | collective-permute-done | bytes 262176 | tf_op jit(solution)/shard_map/ppermute | solution.py:402
  56.6 1.7 %shard_map.19 = f32[4,48,128]{2,1,0:T(8,128)S(1)} custom-call(f32[256,256]{1,0:T(8,128)S(1)} %get-tuple-element.11.t_ref, f32[256,256]{1,0:T(8,128)S(1)} %collective-permute-done.b_ref), custom_call_target="tpu_custom_call" | custom-call | tf_op jit(solution)/shard_map/pallas_call | solution.py:370
  58.3 8.8 %all_to_all.22 = f32[4,48,128]{2,1,0:T(8,128)S(1)} all-to-all(f32[4,48,128]{2,1,0:T(8,128)S(1)} %shard_map.19), channel_id=1, replica_groups=mesh['grp'=16,'far'=8,'near'=4] {'near'}, dimensions={0} | all-to-all | bytes 196608 | tf_op jit(solution)/shard_map/all_to_all | solution.py:385
  67.1 19.8 %all_to_all.23.parts_ref = f32[8,48,128]{2,1,0:T(8,128)S(1)} all-to-all(f32[8,48,128]{2,1,0:T(8,128)S(1)} %broadcast_in_dim.19), channel_id=1, replica_groups=mesh['grp'=16,'far'=8,'near'=4] {'far'}, dimensions={0} | all-to-all | bytes 393216 | tf_op jit(solution)/shard_map/all_to_all | solution.py:390
  86.9 3.5 %shard_map.20 = f32[256,512]{1,0:T(8,128)} custom-call(f32[8,48,128]{2,1,0:T(8,128)S(1)} %all_to_all.23.parts_ref, f32[256,256]{1,0:T(8,128)S(1)} %get-tuple-element.11.t_ref, f32[256,256]{1,0:T(8,128)S(1)} %collective-permute-done.b_ref), custom_call_target="tpu_custom_call" | custom-call | tf_op jit(solution)/shard_map/pallas_call | solution.py:370
  (4 shorter events, 0.0 us)
Async XLA Ops:
  0.0 1.0 %copy-start = (f32[256,512]{1,0:T(8,128)S(1)}, f32[256,512]{1,0:T(8,128)}, u32[]{:S(2)}) copy-start(f32[256,512]{1,0:T(8,128)} %t_ref.1) | copy-start | bytes 1572868
  48.9 7.7 %collective-permute-start = (f32[256,256]{1,0:T(8,128)S(1)}, f32[256,256]{1,0:T(8,128)S(1)}, u32[]{:S(2)}, u32[]{:S(2)}) collective-permute-start(f32[256,256]{1,0:T(8,128)S(1)} %get-tuple-element.12), channel_id=1, source_target_pairs={{0,32},{32,64},{64,96},{96,128},{128,160},{160,192},{192,224},{224... | collective-permute-start | bytes 786440 | tf_op jit(solution)/shard_map/ppermute | solution.py:402

commit v4 on v3

--- a/solution.py
+++ b/solution.py
@@ -186,18 +186,35 @@
     shape = (DIAGS, HALF)
     i = lanes(shape)
     j = i + MID - lax.broadcasted_iota(jnp.int32, shape, 0)
-    i_one, i_more, i_last = i == 1, i >= 2, i == HALF - 1
-    j_one, j_more, j_last = j == 1, j >= 2, j == HALF - 1
-
-    def less(x):
-        return turn_lines(x, -1)
-
-    def more(x):
-        return turn_lines(x, 1)
+    i_none, i_one, i_last = i == 0, i == 1, i == HALF - 1
+    j_none, j_one, j_last = j == 0, j == 1, j == HALF - 1
+    one = lanes((1, HALF))
+    one_none, one_one, one_last = one == 0, one == 1, one == HALF - 1
+
+    def less(x, by=1):
+        return turn_lines(x, -by)
+
+    def more(x, by=1):
+        return turn_lines(x, by)
+
+    def up(x):
+        return turn_lanes(x, 1)
+
+    def down(x):
+        return turn_lanes(x, -1)
+
+    def both_sides(blocks, c_row, s_row, c_col, s_col):
+        tt, tb, bt, bb = blocks
+        tt, tb = c_col * tt - s_col * tb, s_col * tt + c_col * tb
+        bt, bb = c_col * bt - s_col * bb, s_col * bt + c_col * bb
+        tt, bt = c_row * tt - s_row * bt, s_row * tt + c_row * bt
+        tb, bb = c_row * tb - s_row * bb, s_row * tb + c_row * bb
+        return tt, tb, bt, bb
 
     cosines, sines = [], []
+    blocks = tt, tb, bt, bb
+    first, second, coupling = (x[MID : MID + 1] for x in (tt, bb, tb))
     for turn in range(ROUNDS):
-        first, second, coupling = (x[MID : MID + 1] for x in (tt, bb, tb))
         difference = second - first
         direction = jnp.where(difference >= 0, 1.0, -1.0)
         denominator = (
@@ -206,33 +223,55 @@
             + 1e-06 * (first + second)
         )
         tangent = direction * 2.0 * coupling / denominator
-        c = 1.0 / jnp.sqrt(1.0 + tangent * tangent)
+        c = lax.rsqrt(1.0 + tangent * tangent)
         s = tangent * c
         cosines.append(c)
         sines.append(s)
         if turn == ROUNDS - 1:
             break
-        c_row, s_row = jnp.broadcast_to(c, shape), jnp.broadcast_to(s, shape)
-        c_col, s_col = along_columns(c), along_columns(s)
-        tt, tb = c_col * tt - s_col * tb, s_col * tt + c_col * tb
-        bt, bb = c_col * bt - s_col * bb, s_col * bt + c_col * bb
-        tt, bt = c_row * tt - s_row * bt, s_row * tt + c_row * bt
-        tb, bb = c_row * tb - s_row * bb, s_row * tb + c_row * bb
-        tt, tb = (
-            jnp.where(j_more, less(tt), jnp.where(j_one, less(tb), tt)),
-            jnp.where(j_last, tt, more(tb)),
+        here = both_sides([x[MID : MID + 1] for x in blocks], c, s, c, s)
+        next_one = both_sides([x[MID - 1 : MID] for x in blocks], c, s, down(c), down(s))
+        next_two = both_sides([x[MID - 2 : MID - 1] for x in blocks], c, s, turn_lanes(c, -2), turn_lanes(s, -2))
+        first = jnp.where(one_none, here[0], jnp.where(one_one, up(here[3]), up(here[0])))
+        second = jnp.where(one_last, here[0], down(here[3]))
+        coupling = jnp.where(
+            one_none,
+            next_one[1],
+            jnp.where(one_one, up(next_two[3]), jnp.where(one_last, up(next_one[0]), up(next_two[1]))),
         )
-        bt, bb = (
-            jnp.where(j_more, less(bt), jnp.where(j_one, less(bb), bt)),
-            jnp.where(j_last, bt, more(bb)),
+        if turn == ROUNDS - 2:
+            continue
+        tt, tb, bt, bb = both_sides(
+            blocks,
+            jnp.broadcast_to(c, shape),
+            jnp.broadcast_to(s, shape),
+            along_columns(c),
+            along_columns(s),
         )
-        tt, bt = (
-            jnp.where(i_more, turn_lanes(more(tt), 1), jnp.where(i_one, turn_lanes(more(bt), 1), tt)),
-            jnp.where(i_last, tt, turn_lanes(less(bt), -1)),
-        )
-        tb, bb = (
-            jnp.where(i_more, turn_lanes(more(tb), 1), jnp.where(i_one, turn_lanes(more(bb), 1), tb)),
-            jnp.where(i_last, tb, turn_lanes(less(bb), -1)),
+        column, corner = jnp.where(j_none, tb, tt), jnp.where(j_none, bb, bt)
+        blocks = (
+            jnp.where(
+                i_none,
+                jnp.where(j_none, tt, less(column)),
+                jnp.where(j_none, up(more(jnp.where(i_none, bt, tt))), up(jnp.where(i_none, corner, column))),
+            ),
+            jnp.where(
+                i_none,
+                more(tb),
+                jnp.where(j_last, up(more(tt)), up(more(jnp.where(i_none, bb, tb), 2))),
+            ),
+            jnp.where(
+                i_last,
+                less(tt),
+                jnp.where(
+                    j_none, down(less(bt)), jnp.where(j_one, down(less(bb, 2)), down(less(bt, 2)))
+                ),
+            ),
+            jnp.where(
+                i_last,
+                jnp.where(j_last, tt, more(tb)),
+                jnp.where(j_last, down(less(bt)), down(bb)),
+            ),
         )
     return cosines, sines
 

time: 90.7 us -> 89.3 us (0.985)
  Pallas kernels: 9.75 us -> 8.37 us
    pallas_call x4, Pallas kernels: 9.75 us -> 8.37 us  [call(): pl.pallas_call(body, out_shape=shapes, in_specs=[vmem] * len(args), out_s...]
where the time goes in v4:
time: 89.3 us; the launch traced here: 89 us
  blocking collectives  71.8 us (80%)
  Pallas kernels  8.37 us (9%)
  waiting for transfers between devices  5.76 us (6%)
  starting transfers between devices  1.92 us (2%)
  local copies, waits for them, and re-layouts  1.07 us (1%)
    all_to_all x2, blocking collectives, exchanged(): return lax.all_to_all(again, FAR, 0, 0, tiled=True)  51.2 us
    all_to_all x2, blocking collectives, exchanged(): arrived = lax.all_to_all(parts, NEAR, 0, 0, tiled=True)  20.7 us
    pallas_call x4, Pallas kernels, call(): pl.pallas_call(body, out_shape=shapes, in_specs=[vmem] * len(args), out_s...  8.37 us
    ppermute x1, waiting for transfers between devices, per_device(): b = lax.ppermute(b, 'grp', [(i, (i + 1) % groups) for i in range(groups)])  5.76 us
    ppermute x1, starting transfers between devices, per_device(): b = lax.ppermute(b, 'grp', [(i, (i + 1) % groups) for i in range(groups)])  1.92 us
  transfers between devices with their start and end apart: 1, of which 1 were waited for; matrix products, arithmetic and copies ran while one was open for 0% of the time, Pallas kernels for 0%

profile of v4, /device:TPU:8, one launch (start us, length us, event | category | flops | bytes accessed | tf_op | source)
XLA Modules:
  0.0 89.0 jit_solution(14672852053229982750)
XLA Ops:
  0.0 0.0 copy-start
  0.0 1.0 %copy-done = f32[256,512]{1,0:T(8,128)S(1)} copy-done((f32[256,512]{1,0:T(8,128)S(1)}, f32[256,512]{1,0:T(8,128)}, u32[]{:S(2)}) %copy-start) | copy-done | bytes 524312
  1.0 1.8 %shard_map.17 = (f32[4,48,128]{2,1,0:T(8,128)S(1)}, f32[256,256]{1,0:T(8,128)S(1)}) custom-call(f32[256,512]{1,0:T(8,128)S(1)} %copy-done), custom_call_target="tpu_custom_call" | custom-call | tf_op jit(solution)/shard_map/pallas_call | solution.py:409
  2.8 11.9 %all_to_all.20 = f32[4,48,128]{2,1,0:T(8,128)S(1)} all-to-all(f32[4,48,128]{2,1,0:T(8,128)S(1)} %get-tuple-element.9), channel_id=1, replica_groups=mesh['grp'=16,'far'=8,'near'=4] {'near'}, dimensions={0} | all-to-all | bytes 196608 | tf_op jit(solution)/shard_map/all_to_all | solution.py:424
  14.8 31.4 %all_to_all.21.parts_ref = f32[8,48,128]{2,1,0:T(8,128)S(1)} all-to-all(f32[8,48,128]{2,1,0:T(8,128)S(1)} %broadcast_in_dim.17), channel_id=1, replica_groups=mesh['grp'=16,'far'=8,'near'=4] {'far'}, dimensions={0} | all-to-all | bytes 393216 | tf_op jit(solution)/shard_map/all_to_all | solution.py:429
  46.2 2.1 %shard_map.18 = (f32[256,256]{1,0:T(8,128)S(1)}, f32[256,256]{1,0:T(8,128)S(1)}) custom-call(f32[8,48,128]{2,1,0:T(8,128)S(1)} %all_to_all.21.parts_ref, f32[256,512]{1,0:T(8,128)S(1)} %copy-done, f32[256,256]{1,0:T(8,128)S(1)} %get-tuple-element.10.b_ref), custom_call_target="tpu_custom_call" | custom-call | tf_op jit(solution)/shard_map/pallas_call | solution.py:409
  48.2 1.9 %collective-permute-start = (f32[256,256]{1,0:T(8,128)S(1)}, f32[256,256]{1,0:T(8,128)S(1)}, u32[]{:S(2)}, u32[]{:S(2)}) collective-permute-start(f32[256,256]{1,0:T(8,128)S(1)} %get-tuple-element.12), channel_id=1, source_target_pairs={{0,32},{32,64},{64,96},{96,128},{128,160},{160,192},{192,224},{224... | collective-permute-start | bytes 786440 | tf_op jit(solution)/shard_map/ppermute | solution.py:441
  50.2 5.8 %collective-permute-done.b_ref = f32[256,256]{1,0:T(8,128)S(1)} collective-permute-done((f32[256,256]{1,0:T(8,128)S(1)}, f32[256,256]{1,0:T(8,128)S(1)}, u32[]{:S(2)}, u32[]{:S(2)}) %collective-permute-start) | collective-permute-done | bytes 262176 | tf_op jit(solution)/shard_map/ppermute | solution.py:441
  55.9 1.7 %shard_map.19 = f32[4,48,128]{2,1,0:T(8,128)S(1)} custom-call(f32[256,256]{1,0:T(8,128)S(1)} %get-tuple-element.11.t_ref, f32[256,256]{1,0:T(8,128)S(1)} %collective-permute-done.b_ref), custom_call_target="tpu_custom_call" | custom-call | tf_op jit(solution)/shard_map/pallas_call | solution.py:409
  57.6 8.8 %all_to_all.22 = f32[4,48,128]{2,1,0:T(8,128)S(1)} all-to-all(f32[4,48,128]{2,1,0:T(8,128)S(1)} %shard_map.19), channel_id=1, replica_groups=mesh['grp'=16,'far'=8,'near'=4] {'near'}, dimensions={0} | all-to-all | bytes 196608 | tf_op jit(solution)/shard_map/all_to_all | solution.py:424
  66.4 19.8 %all_to_all.23.parts_ref = f32[8,48,128]{2,1,0:T(8,128)S(1)} all-to-all(f32[8,48,128]{2,1,0:T(8,128)S(1)} %broadcast_in_dim.19), channel_id=1, replica_groups=mesh['grp'=16,'far'=8,'near'=4] {'far'}, dimensions={0} | all-to-all | bytes 393216 | tf_op jit(solution)/shard_map/all_to_all | solution.py:429
  86.2 2.8 %shard_map.20 = f32[256,512]{1,0:T(8,128)} custom-call(f32[8,48,128]{2,1,0:T(8,128)S(1)} %all_to_all.23.parts_ref, f32[256,256]{1,0:T(8,128)S(1)} %get-tuple-element.11.t_ref, f32[256,256]{1,0:T(8,128)S(1)} %collective-permute-done.b_ref), custom_call_target="tpu_custom_call" | custom-call | tf_op jit(solution)/shard_map/pallas_call | solution.py:409
  (4 shorter events, 0.0 us)
Async XLA Ops:
  0.0 1.0 %copy-start = (f32[256,512]{1,0:T(8,128)S(1)}, f32[256,512]{1,0:T(8,128)}, u32[]{:S(2)}) copy-start(f32[256,512]{1,0:T(8,128)} %t_ref.1) | copy-start | bytes 1572868
  48.2 7.7 %collective-permute-start = (f32[256,256]{1,0:T(8,128)S(1)}, f32[256,256]{1,0:T(8,128)S(1)}, u32[]{:S(2)}, u32[]{:S(2)}) collective-permute-start(f32[256,256]{1,0:T(8,128)S(1)} %get-tuple-element.12), channel_id=1, source_target_pairs={{0,32},{32,64},{64,96},{96,128},{128,160},{160,192},{192,224},{224... | collective-permute-start | bytes 786440 | tf_op jit(solution)/shard_map/ppermute | solution.py:441

commit v5 on v4

--- a/solution.py
+++ b/solution.py
@@ -91,17 +91,34 @@
     return ref[at, :128], ref[at, 128:256]
 
 
-def band_of(load, count, out_ref, sums_ref):
-    def over_rows(step, n, width):
-        zeros = tuple(jnp.zeros((8, 128), f32) for _ in range(n * width))
-        return lax.fori_loop(0, count, lambda k, sums: step(*load(k), sums), zeros, unroll=16)
-
-    def with_top(t, b, sums):
+def over_rows(load, count, step, n):
+    zeros = (jnp.zeros((8, 128), f32),) * n
+    return lax.fori_loop(0, count, lambda k, sums: step(*load(k), sums), zeros, unroll=16)
+
+
+def top_band_of(load, count, top_ref):
+    def step(t, sums):
         new = []
         for d in range(0, REACH + 1, 2):
             shifted = ahead(t, d) if d else t
-            for left in (t, b) if d else (t,):
-                new += [left[h] * shifted[h] for h in range(2)]
+            new += [t[h] * shifted[h] for h in range(2)]
+        return tuple(x + y for x, y in zip(sums, new))
+
+    sums = over_rows(lambda k: (load(k),), count, step, 12)
+    for h in range(2):
+        for j in range(6):
+            top_ref[pl.ds(48 * h + 8 * j, 8), :] = sums[2 * j + h]
+
+
+def band_of(load, count, out_ref, sums_ref, top_ref=None):
+    def with_top(t, b, sums):
+        new = []
+        for d in range(2 if top_ref is not None else 0, REACH + 1, 2):
+            shifted = ahead(t, d) if d else t
+            if top_ref is None:
+                new += [t[h] * shifted[h] for h in range(2)]
+            if d:
+                new += [b[h] * shifted[h] for h in range(2)]
         return tuple(x + y for x, y in zip(sums, new))
 
     def with_bottom(t, b, sums):
@@ -120,18 +137,25 @@
     def keep(line, value):
         sums_ref[pl.ds(8 * line, 8), :] = value
 
-    sums = over_rows(with_top, 11, 2)
-    for h in range(2):
-        keep(24 * h, sums[h])
-        for j in range(1, 6):
-            keep(24 * h + j, sums[4 * j - 2 + h])
-            keep(24 * h + 17 + j, sums[4 * j + h])
-    sums = over_rows(with_bottom, 12, 2)
+    if top_ref is not None:
+        sums = over_rows(load, count, with_top, 10)
+        for h in range(2):
+            sums_ref[pl.ds(8 * 24 * h, 48), :] = top_ref[pl.ds(48 * h, 48), :]
+            for j in range(1, 6):
+                keep(24 * h + 17 + j, sums[2 * j - 2 + h])
+    else:
+        sums = over_rows(load, count, with_top, 22)
+        for h in range(2):
+            keep(24 * h, sums[h])
+            for j in range(1, 6):
+                keep(24 * h + j, sums[4 * j - 2 + h])
+                keep(24 * h + 17 + j, sums[4 * j + h])
+    sums = over_rows(load, count, with_bottom, 24)
     for h in range(2):
         for j in range(6):
             keep(24 * h + 6 + j, sums[4 * j + h])
             keep(24 * h + 12 + j, sums[4 * j + 2 + h])
-    sums = over_rows(at_ends, 5, 1)
+    sums = over_rows(load, count, at_ends, 5)
     for j in range(5):
         keep(LINES + j, sums[j])
     for line in (WIDE, LINES - 1, LINES + 5, LINES + 6, LINES + 7):
@@ -365,27 +389,50 @@
     band_of(load, p_ref.shape[0] // 8, out_ref, sums_ref)
 
 
-def second_band(t_ref, b_ref, out_ref, sums_ref):
+def first_angles(parts_ref, turns_ref, x_ref):
+    cosines, sines = angles_of(parts_ref, x_ref)
+    turns_ref[...] = jnp.zeros_like(turns_ref)
+    for k in range(ROUNDS):
+        turns_ref[k : k + 1, :] = cosines[k]
+        turns_ref[8 + k : 9 + k, :] = sines[k]
+
+
+def given(turns_ref):
+    return (
+        [turns_ref[k : k + 1, :] for k in range(ROUNDS)],
+        [turns_ref[8 + k : 9 + k, :] for k in range(ROUNDS)],
+    )
+
+
+def own_turn(turns_ref, p_ref, b_ref, t_out, top_ref):
     def load(k):
+        at = rows_at(k, CHUNK)
+        return halves(p_ref, at), halves(b_ref, at)
+
+    def store(k, t, b):
+        at = rows_at(k, CHUNK)
+        t_out[at, :128], t_out[at, 128:] = retreated_top(t, b)
+
+    turned_chunks(load, store, t_out.shape[0] // CHUNK, CHUNK, *given(turns_ref))
+    top_band_of(lambda k: halves(t_out, rows_at(k, 8)), t_out.shape[0] // 8, top_ref)
+
+
+def arrived_turn(turns_ref, p_ref, t_ref, top_ref, b_out, out_ref, sums_ref):
+    def load(k):
+        at = rows_at(k, CHUNK)
+        return halves(p_ref, at), mirrored(p_ref[at, 256:384], p_ref[at, 384:])
+
+    def store(k, t, b):
+        at = rows_at(k, CHUNK)
+        b_out[at, :128], b_out[at, 128:] = retreated_bottom(t, b)
+
+    turned_chunks(load, store, t_ref.shape[0] // CHUNK, CHUNK, *given(turns_ref))
+
+    def rows(k):
         at = rows_at(k, 8)
-        return halves(t_ref, at), halves(b_ref, at)
-
-    band_of(load, t_ref.shape[0] // 8, out_ref, sums_ref)
-
-
-def first_turn(parts_ref, t_ref, b_ref, t_out, b_out, x_ref):
-    cosines, sines = angles_of(parts_ref, x_ref)
-
-    def load(k):
-        at = rows_at(k, CHUNK)
-        return halves(t_ref, at), halves(b_ref, at)
-
-    def store(k, t, b):
-        at = rows_at(k, CHUNK)
-        t_out[at, :128], t_out[at, 128:] = retreated_top(t, b)
-        b_out[at, :128], b_out[at, 128:] = retreated_bottom(t, b)
-
-    turned_chunks(load, store, t_ref.shape[0] // CHUNK, CHUNK, cosines, sines)
+        return halves(t_ref, at), halves(b_out, at)
+
+    band_of(rows, t_ref.shape[0] // 8, out_ref, sums_ref, top_ref)
 
 
 def second_turn(parts_ref, t_ref, b_ref, out_ref, x_ref):
@@ -433,13 +480,20 @@
 STATE = [(4, DIAGS, HALF)]
 
 
+TOP = (2 * 6 * 8, 128)
+TURNS = (16, HALF)
+
+
 def per_device(snapshots, near, far, groups):
     rows = snapshots.shape[0]
     square, band = (rows, HALF), (near, LINES, 128)
+    onward = [(i, (i + 1) % groups) for i in range(groups)]
+    raw = lax.ppermute(snapshots, "grp", onward)
     parts, b = call(first_band, [band, square], [snapshots], SUMS)
-    t, b = call(first_turn, [square, square], [exchanged(parts, near, far), snapshots, b], STATE)
-    b = lax.ppermute(b, "grp", [(i, (i + 1) % groups) for i in range(groups)])
-    (parts,) = call(second_band, [band], [t, b], SUMS)
+    (turns,) = call(first_angles, [TURNS], [exchanged(parts, near, far)], STATE)
+    their_turns = lax.ppermute(turns, "grp", onward)
+    t, top = call(own_turn, [square, TOP], [turns, snapshots, b])
+    b, parts = call(arrived_turn, [square, band], [their_turns, raw, t, top], SUMS)
     (out,) = call(second_turn, [(rows, 2 * HALF)], [exchanged(parts, near, far), t, b], STATE)
     return out
 

time: 89.3 us -> 89.2 us (level)
  blocking collectives: 71.8 us -> 41.5 us
  starting transfers between devices: 1.92 us -> 18 us
  waiting for transfers between devices: 5.76 us -> 16.9 us
  Pallas kernels: 8.37 us -> 10.5 us
    all_to_all x2 -> x1, blocking collectives: 51.2 us -> 20.7 us  [exchanged(): return lax.all_to_all(again, FAR, 0, 0, tiled=True)]
    all_to_all x0 -> x1, waiting for transfers between devices: none -> 15.5 us  [exchanged(): return lax.all_to_all(again, FAR, 0, 0, tiled=True)]
    all_to_all x0 -> x1, starting transfers between devices: none -> 14.2 us  [exchanged(): return lax.all_to_all(again, FAR, 0, 0, tiled=True)]
    ppermute x1 -> x2, waiting for transfers between devices: 5.76 us -> 1.41 us  [the longest x1 1.4 us: per_device(): their_turns = lax.ppermute(turns, 'grp', onward)]
    pallas_call x4 -> x5, Pallas kernels: 8.37 us -> 10.5 us  [call(): pl.pallas_call(body, out_shape=shapes, in_specs=[vmem] * len(args), out_s...]
    ppermute x1 -> x2, starting transfers between devices: 1.92 us -> 3.84 us  [the longest x1 1.92 us: per_device(): raw = lax.ppermute(snapshots, 'grp', onward)]
  transfers between devices with their start and end apart: 1 -> 3, of which waited for: 1 -> 2; matrix products, arithmetic and copies ran while one was open for 0% -> 0% of each run, Pallas kernels for 0% -> 3%
where the time goes in v5:
time: 89.2 us; the launch traced here: 88.7 us
  blocking collectives  41.5 us (47%)
  starting transfers between devices  18 us (20%)
  waiting for transfers between devices  16.9 us (19%)
  Pallas kernels  10.5 us (12%)
  local copies, waits for them, and re-layouts  1.75 us (2%)
    all_to_all x2, blocking collectives, exchanged(): arrived = lax.all_to_all(parts, NEAR, 0, 0, tiled=True)  20.8 us
    all_to_all x1, blocking collectives, exchanged(): return lax.all_to_all(again, FAR, 0, 0, tiled=True)  20.7 us
    all_to_all x1, waiting for transfers between devices, exchanged(): return lax.all_to_all(again, FAR, 0, 0, tiled=True)  15.5 us
    all_to_all x1, starting transfers between devices, exchanged(): return lax.all_to_all(again, FAR, 0, 0, tiled=True)  14.2 us
    pallas_call x5, Pallas kernels, call(): pl.pallas_call(body, out_shape=shapes, in_specs=[vmem] * len(args), out_s...  10.5 us
    ppermute x1, starting transfers between devices, per_device(): raw = lax.ppermute(snapshots, 'grp', onward)  1.92 us
    ppermute x1, starting transfers between devices, per_device(): their_turns = lax.ppermute(turns, 'grp', onward)  1.92 us
  transfers between devices with their start and end apart: 3, of which 2 were waited for; matrix products, arithmetic and copies ran while one was open for 0% of the time, Pallas kernels for 3%

profile of v5, /device:TPU:8, one launch (start us, length us, event | category | flops | bytes accessed | tf_op | source)
XLA Modules:
  0.0 88.7 jit_solution(13668825822183422117)
XLA Ops:
  0.0 0.0 copy-start
  0.0 1.0 %copy-done = f32[256,512]{1,0:T(8,128)S(1)} copy-done((f32[256,512]{1,0:T(8,128)S(1)}, f32[256,512]{1,0:T(8,128)}, u32[]{:S(2)}) %copy-start) | copy-done | bytes 524312
  1.0 1.8 %shard_map.17 = (f32[4,48,128]{2,1,0:T(8,128)S(1)}, f32[256,256]{1,0:T(8,128)S(1)}) custom-call(f32[256,512]{1,0:T(8,128)S(1)} %copy-done), custom_call_target="tpu_custom_call" | custom-call | tf_op jit(solution)/shard_map/pallas_call | solution.py:456
  2.8 0.0 copy-start.1
  2.8 12.0 %all_to_all.20 = f32[4,48,128]{2,1,0:T(8,128)S(1)} all-to-all(f32[4,48,128]{2,1,0:T(8,128)S(1)} %get-tuple-element.11), channel_id=1, replica_groups=mesh['grp'=16,'far'=8,'near'=4] {'near'}, dimensions={0} | all-to-all | bytes 196608 | tf_op jit(solution)/shard_map/all_to_all | solution.py:471
  14.9 0.7 broadcast_in_dim.17
  15.6 14.2 %all-to-all-start.1 = ((f32[8,48,128]{2,1,0:T(8,128)}), f32[8,48,128]{2,1,0:T(8,128)S(1)}, u32[]{:S(2)}, u32[]{:S(2)}) async-start(f32[8,48,128]{2,1,0:T(8,128)} %broadcast_in_dim.17), calls=%async_computation.1 | async-start | bytes 393216 | tf_op jit(solution)/shard_map/all_to_all | solution.py:476
  29.7 0.0 copy-done.1
  29.8 1.9 %collective-permute-start.1 = (f32[256,512]{1,0:T(8,128)S(1)}, f32[256,512]{1,0:T(8,128)S(1)}, u32[]{:S(2)}, u32[]{:S(2)}) collective-permute-start(f32[256,512]{1,0:T(8,128)S(1)} %copy-done.1), channel_id=1, source_target_pairs={{0,32},{32,64},{64,96},{96,128},{128,160},{160,192},{192,224},{224... | collective-permute-start | bytes 1572872 | tf_op jit(solution)/shard_map/ppermute | solution.py:491
  31.7 15.5 %all-to-all-done.1.parts_ref = f32[8,48,128]{2,1,0:T(8,128)S(1)} async-done(((f32[8,48,128]{2,1,0:T(8,128)}), f32[8,48,128]{2,1,0:T(8,128)S(1)}, u32[]{:S(2)}, u32[]{:S(2)}) %all-to-all-start.1) | async-done | bytes 196640 | tf_op jit(solution)/shard_map/all_to_all | solution.py:476
  47.2 1.2 %shard_map.18.turns_ref = f32[16,256]{1,0:T(8,128)S(1)} custom-call(f32[8,48,128]{2,1,0:T(8,128)S(1)} %all-to-all-done.1.parts_ref), custom_call_target="tpu_custom_call" | custom-call | tf_op jit(solution)/shard_map/pallas_call | solution.py:456
  48.3 1.9 %collective-permute-start = (f32[16,256]{1,0:T(8,128)S(1)}, f32[16,256]{1,0:T(8,128)S(1)}, u32[]{:S(2)}, u32[]{:S(2)}) collective-permute-start(f32[16,256]{1,0:T(8,128)S(1)} %shard_map.18.turns_ref), channel_id=1, source_target_pairs={{0,32},{32,64},{64,96},{96,128},{128,160},{160,192},{192,224},{224... | collective-permute-start | bytes 49160 | tf_op jit(solution)/shard_map/ppermute | solution.py:494
  50.3 1.7 %shard_map.19 = (f32[256,256]{1,0:T(8,128)S(1)}, f32[96,128]{1,0:T(8,128)S(1)}) custom-call(f32[16,256]{1,0:T(8,128)S(1)} %shard_map.18.turns_ref, f32[256,512]{1,0:T(8,128)S(1)} %copy-done.1, f32[256,256]{1,0:T(8,128)S(1)} %get-tuple-element.12.b_ref), custom_call_target="tpu_custom_call" | custom-call | tf_op jit(solution)/shard_map/pallas_call | solution.py:456
  52.0 0.0 collective-permute-done.1.p_ref
  52.0 1.4 %collective-permute-done.turns_ref = f32[16,256]{1,0:T(8,128)S(1)} collective-permute-done((f32[16,256]{1,0:T(8,128)S(1)}, f32[16,256]{1,0:T(8,128)S(1)}, u32[]{:S(2)}, u32[]{:S(2)}) %collective-permute-start) | collective-permute-done | bytes 16416 | tf_op jit(solution)/shard_map/ppermute | solution.py:494
  53.4 3.0 %shard_map.20 = (f32[256,256]{1,0:T(8,128)S(1)}, f32[4,48,128]{2,1,0:T(8,128)S(1)}) custom-call(f32[16,256]{1,0:T(8,128)S(1)} %collective-permute-done.turns_ref, f32[256,512]{1,0:T(8,128)S(1)} %collective-permute-done.1.p_ref, f32[256,256]{1,0:T(8,128)S(1)} %get-tuple-element.13.t_ref, f32[96,128]{1,0:T(8,128)S(1)} %get-tuple-element.14.top_ref), custom_call_target="tpu_custom_call" | custom-call | tf_op jit(solution)/shard_map/pallas_call | solution.py:456
  56.3 8.8 %all_to_all.21 = f32[4,48,128]{2,1,0:T(8,128)S(1)} all-to-all(f32[4,48,128]{2,1,0:T(8,128)S(1)} %get-tuple-element.15), channel_id=1, replica_groups=mesh['grp'=16,'far'=8,'near'=4] {'near'}, dimensions={0} | all-to-all | bytes 196608 | tf_op jit(solution)/shard_map/all_to_all | solution.py:471
  65.2 20.7 %all_to_all.22.parts_ref = f32[8,48,128]{2,1,0:T(8,128)S(1)} all-to-all(f32[8,48,128]{2,1,0:T(8,128)S(1)} %broadcast_in_dim.19), channel_id=1, replica_groups=mesh['grp'=16,'far'=8,'near'=4] {'far'}, dimensions={0} | all-to-all | bytes 393216 | tf_op jit(solution)/shard_map/all_to_all | solution.py:476
  85.9 2.8 %shard_map.21 = f32[256,512]{1,0:T(8,128)} custom-call(f32[8,48,128]{2,1,0:T(8,128)S(1)} %all_to_all.22.parts_ref, f32[256,256]{1,0:T(8,128)S(1)} %get-tuple-element.13.t_ref, f32[256,256]{1,0:T(8,128)S(1)} %get-tuple-element.16.b_ref), custom_call_target="tpu_custom_call" | custom-call | tf_op jit(solution)/shard_map/pallas_call | solution.py:456
  (3 shorter events, 0.0 us)
Async XLA Ops:
  0.0 1.0 %copy-start = (f32[256,512]{1,0:T(8,128)S(1)}, f32[256,512]{1,0:T(8,128)}, u32[]{:S(2)}) copy-start(f32[256,512]{1,0:T(8,128)} %p_ref.3) | copy-start | bytes 1572868
  2.8 26.9 %copy-start.1 = (f32[256,512]{1,0:T(8,128)S(1)}, f32[256,512]{1,0:T(8,128)}, u32[]{:S(2)}) copy-start(f32[256,512]{1,0:T(8,128)} %p_ref.3) | copy-start | bytes 1572868
  15.6 31.6 %all-to-all-start.1 = ((f32[8,48,128]{2,1,0:T(8,128)}), f32[8,48,128]{2,1,0:T(8,128)S(1)}, u32[]{:S(2)}, u32[]{:S(2)}) async-start(f32[8,48,128]{2,1,0:T(8,128)} %broadcast_in_dim.17), calls=%async_computation.1 | async-start | bytes 393216 | tf_op jit(solution)/shard_map/all_to_all | solution.py:476
  29.8 22.2 %collective-permute-start.1 = (f32[256,512]{1,0:T(8,128)S(1)}, f32[256,512]{1,0:T(8,128)S(1)}, u32[]{:S(2)}, u32[]{:S(2)}) collective-permute-start(f32[256,512]{1,0:T(8,128)S(1)} %copy-done.1), channel_id=1, source_target_pairs={{0,32},{32,64},{64,96},{96,128},{128,160},{160,192},{192,224},{224... | collective-permute-start | bytes 1572872 | tf_op jit(solution)/shard_map/ppermute | solution.py:491
  48.3 5.1 %collective-permute-start = (f32[16,256]{1,0:T(8,128)S(1)}, f32[16,256]{1,0:T(8,128)S(1)}, u32[]{:S(2)}, u32[]{:S(2)}) collective-permute-start(f32[16,256]{1,0:T(8,128)S(1)} %shard_map.18.turns_ref), channel_id=1, source_target_pairs={{0,32},{32,64},{64,96},{96,128},{128,160},{160,192},{192,224},{224... | collective-permute-start | bytes 49160 | tf_op jit(solution)/shard_map/ppermute | solution.py:494

commit v6 on v5

--- a/solution.py
+++ b/solution.py
@@ -1,5 +1,3 @@
-import functools
-
 import jax
 import jax.numpy as jnp
 from jax import lax
@@ -464,16 +462,19 @@
     )(*args)
 
 
-NEAR, FAR = "near", "far"
-
-
-def exchanged(parts, near, far):
-    arrived = lax.all_to_all(parts, NEAR, 0, 0, tiled=True)
+ROW_AXES = ("z3", "z2", "z1", "z0", "side")
+FIRST_SUM = (("z1", "z0", "side"), ("z3", "z2"))
+SECOND_SUM = (("z0", "side"), ("z3", "z2", "z1"))
+
+
+def exchanged(parts, stages):
+    near, far = stages
+    arrived = lax.all_to_all(parts, near, 0, 0, tiled=True)
     total = arrived[0]
-    for k in range(1, near):
+    for k in range(1, arrived.shape[0]):
         total = total + arrived[k]
-    again = jnp.broadcast_to(total[None], (far, *total.shape))
-    return lax.all_to_all(again, FAR, 0, 0, tiled=True)
+    again = jnp.broadcast_to(total[None], (lax.axis_size(far), *total.shape))
+    return lax.all_to_all(again, far, 0, 0, tiled=True)
 
 
 SUMS = [(8 * LINES + 64, 128)]
@@ -484,24 +485,24 @@
 TURNS = (16, HALF)
 
 
-def per_device(snapshots, near, far, groups):
+def per_device(snapshots):
     rows = snapshots.shape[0]
-    square, band = (rows, HALF), (near, LINES, 128)
+    square = (rows, HALF)
+    first, second = ((lax.axis_size(stages[0]), LINES, 128) for stages in (FIRST_SUM, SECOND_SUM))
+    groups = lax.axis_size("grp")
     onward = [(i, (i + 1) % groups) for i in range(groups)]
     raw = lax.ppermute(snapshots, "grp", onward)
-    parts, b = call(first_band, [band, square], [snapshots], SUMS)
-    (turns,) = call(first_angles, [TURNS], [exchanged(parts, near, far)], STATE)
+    parts, b = call(first_band, [first, square], [snapshots], SUMS)
+    (turns,) = call(first_angles, [TURNS], [exchanged(parts, FIRST_SUM)], STATE)
     their_turns = lax.ppermute(turns, "grp", onward)
     t, top = call(own_turn, [square, TOP], [turns, snapshots, b])
-    b, parts = call(arrived_turn, [square, band], [their_turns, raw, t, top], SUMS)
-    (out,) = call(second_turn, [(rows, 2 * HALF)], [exchanged(parts, near, far), t, b], STATE)
+    b, parts = call(arrived_turn, [square, second], [their_turns, raw, t, top], SUMS)
+    (out,) = call(second_turn, [(rows, 2 * HALF)], [exchanged(parts, SECOND_SUM), t, b], STATE)
     return out
 
 
 def solution(mesh):
-    groups, rows = mesh.shape["grp"], mesh.shape["row"]
-    near, far = 4, rows // 4
-    fine = Mesh(mesh.devices.reshape(groups, far, near), ("grp", "far", "near"))
-    placed = P(("far", "near"), "grp")
-    body = functools.partial(per_device, near=near, far=far, groups=groups)
-    return jax.shard_map(body, mesh=fine, in_specs=(placed,), out_specs=placed, check_vma=False)
+    sizes = (mesh.shape["grp"], mesh.shape["row"] // 16, 2, 2, 2, 2)
+    fine = Mesh(mesh.devices.reshape(sizes), ("grp", *ROW_AXES))
+    placed = P(ROW_AXES, "grp")
+    return jax.shard_map(per_device, mesh=fine, in_specs=(placed,), out_specs=placed, check_vma=False)

time: 89.2 us -> 88.6 us (level)
  blocking collectives: 41.5 us -> 54.8 us
  waiting for transfers between devices: 16.9 us -> 8.93 us
  starting transfers between devices: 18 us -> 12.2 us
    all_to_all x3, blocking collectives: 41.5 us -> 54.8 us  [the longest x2 45.7 us: exchanged(): return lax.all_to_all(again, far, 0, 0, tiled=True)]
    all_to_all x1, waiting for transfers between devices: 15.5 us -> 7.52 us  [exchanged(): arrived = lax.all_to_all(parts, near, 0, 0, tiled=True)]
    all_to_all x1, starting transfers between devices: 14.2 us -> 8.36 us  [exchanged(): arrived = lax.all_to_all(parts, near, 0, 0, tiled=True)]
where the time goes in v6:
time: 88.6 us; the launch traced here: 88.2 us
  blocking collectives  54.8 us (62%)
  starting transfers between devices  12.2 us (14%)
  Pallas kernels  11.1 us (13%)
  waiting for transfers between devices  8.93 us (10%)
  local copies, waits for them, and re-layouts  1.07 us (1%)
    all_to_all x2, blocking collectives, exchanged(): return lax.all_to_all(again, far, 0, 0, tiled=True)  45.7 us
    pallas_call x5, Pallas kernels, call(): pl.pallas_call(body, out_shape=shapes, in_specs=[vmem] * len(args), out_s...  11.1 us
    all_to_all x1, blocking collectives, exchanged(): arrived = lax.all_to_all(parts, near, 0, 0, tiled=True)  9.1 us
    all_to_all x1, starting transfers between devices, exchanged(): arrived = lax.all_to_all(parts, near, 0, 0, tiled=True)  8.36 us
    all_to_all x1, waiting for transfers between devices, exchanged(): arrived = lax.all_to_all(parts, near, 0, 0, tiled=True)  7.52 us
    ppermute x1, starting transfers between devices, per_device(): raw = lax.ppermute(snapshots, 'grp', onward)  1.92 us
    ppermute x1, starting transfers between devices, per_device(): their_turns = lax.ppermute(turns, 'grp', onward)  1.92 us
  transfers between devices with their start and end apart: 3, of which 2 were waited for; matrix products, arithmetic and copies ran while one was open for 0% of the time, Pallas kernels for 3%

profile of v6, /device:TPU:8, one launch (start us, length us, event | category | flops | bytes accessed | tf_op | source)
XLA Modules:
  0.0 88.2 jit_solution(8624717656545602405)
XLA Ops:
  0.0 0.0 copy-start
  0.0 1.0 %copy-done = f32[256,512]{1,0:T(8,128)S(1)} copy-done((f32[256,512]{1,0:T(8,128)S(1)}, f32[256,512]{1,0:T(8,128)}, u32[]{:S(2)}) %copy-start) | copy-done | bytes 524312
  1.0 0.0 copy-start.1
  1.0 2.5 %shard_map.17 = (f32[8,48,128]{2,1,0:T(8,128)}, f32[256,256]{1,0:T(8,128)S(1)}) custom-call(f32[256,512]{1,0:T(8,128)S(1)} %copy-done), custom_call_target="tpu_custom_call" | custom-call | tf_op jit(solution)/shard_map/pallas_call | solution.py:454
  3.5 8.4 %all-to-all-start = ((f32[8,48,128]{2,1,0:T(8,128)}), f32[8,48,128]{2,1,0:T(8,128)S(1)}, u32[]{:S(2)}, u32[]{:S(2)}) async-start(f32[8,48,128]{2,1,0:T(8,128)} %get-tuple-element.11), calls=%async_computation | async-start | bytes 393216 | tf_op jit(solution)/shard_map/all_to_all | solution.py:472
  11.9 0.0 copy-done.1
  11.9 1.9 %collective-permute-start.1 = (f32[256,512]{1,0:T(8,128)S(1)}, f32[256,512]{1,0:T(8,128)S(1)}, u32[]{:S(2)}, u32[]{:S(2)}) collective-permute-start(f32[256,512]{1,0:T(8,128)S(1)} %copy-done.1), channel_id=1, source_target_pairs={{0,32},{32,64},{64,96},{96,128},{128,160},{160,192},{192,224},{224... | collective-permute-start | bytes 1572872 | tf_op jit(solution)/shard_map/ppermute | solution.py:494
  13.8 7.5 %all-to-all-done = f32[8,48,128]{2,1,0:T(8,128)S(1)} async-done(((f32[8,48,128]{2,1,0:T(8,128)}), f32[8,48,128]{2,1,0:T(8,128)S(1)}, u32[]{:S(2)}, u32[]{:S(2)}) %all-to-all-start) | async-done | bytes 196640 | tf_op jit(solution)/shard_map/all_to_all | solution.py:472
  21.4 25.5 %all_to_all.20.parts_ref = f32[4,48,128]{2,1,0:T(8,128)S(1)} all-to-all(f32[4,48,128]{2,1,0:T(8,128)S(1)} %broadcast_in_dim.17), channel_id=1, replica_groups=mesh['grp'=16,'z3'=2,'z2'=2,'z1'=2,'z0'=2,'side'=2] {'z3','z2'}, dimensions={0} | all-to-all | bytes 196608 | tf_op jit(solution)/shard_map/all_to_all | solution.py:477
  46.8 1.2 %shard_map.18.turns_ref = f32[16,256]{1,0:T(8,128)S(1)} custom-call(f32[4,48,128]{2,1,0:T(8,128)S(1)} %all_to_all.20.parts_ref), custom_call_target="tpu_custom_call" | custom-call | tf_op jit(solution)/shard_map/pallas_call | solution.py:454
  48.0 1.9 %collective-permute-start = (f32[16,256]{1,0:T(8,128)S(1)}, f32[16,256]{1,0:T(8,128)S(1)}, u32[]{:S(2)}, u32[]{:S(2)}) collective-permute-start(f32[16,256]{1,0:T(8,128)S(1)} %shard_map.18.turns_ref), channel_id=1, source_target_pairs={{0,32},{32,64},{64,96},{96,128},{128,160},{160,192},{192,224},{224... | collective-permute-start | bytes 49160 | tf_op jit(solution)/shard_map/ppermute | solution.py:497
  49.9 1.7 %shard_map.19 = (f32[256,256]{1,0:T(8,128)S(1)}, f32[96,128]{1,0:T(8,128)S(1)}) custom-call(f32[16,256]{1,0:T(8,128)S(1)} %shard_map.18.turns_ref, f32[256,512]{1,0:T(8,128)S(1)} %copy-done.1, f32[256,256]{1,0:T(8,128)S(1)} %get-tuple-element.12.b_ref), custom_call_target="tpu_custom_call" | custom-call | tf_op jit(solution)/shard_map/pallas_call | solution.py:454
  51.6 0.0 collective-permute-done.1.p_ref
  51.7 1.4 %collective-permute-done.turns_ref = f32[16,256]{1,0:T(8,128)S(1)} collective-permute-done((f32[16,256]{1,0:T(8,128)S(1)}, f32[16,256]{1,0:T(8,128)S(1)}, u32[]{:S(2)}, u32[]{:S(2)}) %collective-permute-start) | collective-permute-done | bytes 16416 | tf_op jit(solution)/shard_map/ppermute | solution.py:497
  53.1 3.0 %shard_map.20 = (f32[256,256]{1,0:T(8,128)S(1)}, f32[4,48,128]{2,1,0:T(8,128)S(1)}) custom-call(f32[16,256]{1,0:T(8,128)S(1)} %collective-permute-done.turns_ref, f32[256,512]{1,0:T(8,128)S(1)} %collective-permute-done.1.p_ref, f32[256,256]{1,0:T(8,128)S(1)} %get-tuple-element.13.t_ref, f32[96,128]{1,0:T(8,128)S(1)} %get-tuple-element.14.top_ref), custom_call_target="tpu_custom_call" | custom-call | tf_op jit(solution)/shard_map/pallas_call | solution.py:454
  56.0 9.1 %all_to_all.21 = f32[4,48,128]{2,1,0:T(8,128)S(1)} all-to-all(f32[4,48,128]{2,1,0:T(8,128)S(1)} %get-tuple-element.15), channel_id=1, replica_groups=mesh['grp'=16,'z3'=2,'z2'=2,'z1'=2,'z0'=2,'side'=2] {'z0','side'}, dimensions={0} | all-to-all | bytes 196608 | tf_op jit(solution)/shard_map/all_to_all | solution.py:472
  65.1 20.2 %all_to_all.22.parts_ref = f32[8,48,128]{2,1,0:T(8,128)S(1)} all-to-all(f32[8,48,128]{2,1,0:T(8,128)S(1)} %broadcast_in_dim.19), channel_id=1, replica_groups=mesh['grp'=16,'z3'=2,'z2'=2,'z1'=2,'z0'=2,'side'=2] {'z3','z2','z1'}, dimensions={0} | all-to-all | bytes 393216 | tf_op jit(solution)/shard_map/all_to_all | solution.py:477
  85.3 2.8 %shard_map.21 = f32[256,512]{1,0:T(8,128)} custom-call(f32[8,48,128]{2,1,0:T(8,128)S(1)} %all_to_all.22.parts_ref, f32[256,256]{1,0:T(8,128)S(1)} %get-tuple-element.13.t_ref, f32[256,256]{1,0:T(8,128)S(1)} %get-tuple-element.16.b_ref), custom_call_target="tpu_custom_call" | custom-call | tf_op jit(solution)/shard_map/pallas_call | solution.py:454
  (4 shorter events, 0.0 us)
Async XLA Ops:
  0.0 1.0 %copy-start = (f32[256,512]{1,0:T(8,128)S(1)}, f32[256,512]{1,0:T(8,128)}, u32[]{:S(2)}) copy-start(f32[256,512]{1,0:T(8,128)} %p_ref.3) | copy-start | bytes 1572868
  1.0 10.8 %copy-start.1 = (f32[256,512]{1,0:T(8,128)S(1)}, f32[256,512]{1,0:T(8,128)}, u32[]{:S(2)}) copy-start(f32[256,512]{1,0:T(8,128)} %p_ref.3) | copy-start | bytes 1572868
  3.5 17.8 %all-to-all-start = ((f32[8,48,128]{2,1,0:T(8,128)}), f32[8,48,128]{2,1,0:T(8,128)S(1)}, u32[]{:S(2)}, u32[]{:S(2)}) async-start(f32[8,48,128]{2,1,0:T(8,128)} %get-tuple-element.11), calls=%async_computation | async-start | bytes 393216 | tf_op jit(solution)/shard_map/all_to_all | solution.py:472
  11.9 39.8 %collective-permute-start.1 = (f32[256,512]{1,0:T(8,128)S(1)}, f32[256,512]{1,0:T(8,128)S(1)}, u32[]{:S(2)}, u32[]{:S(2)}) collective-permute-start(f32[256,512]{1,0:T(8,128)S(1)} %copy-done.1), channel_id=1, source_target_pairs={{0,32},{32,64},{64,96},{96,128},{128,160},{160,192},{192,224},{224... | collective-permute-start | bytes 1572872 | tf_op jit(solution)/shard_map/ppermute | solution.py:494
  48.0 5.1 %collective-permute-start = (f32[16,256]{1,0:T(8,128)S(1)}, f32[16,256]{1,0:T(8,128)S(1)}, u32[]{:S(2)}, u32[]{:S(2)}) collective-permute-start(f32[16,256]{1,0:T(8,128)S(1)} %shard_map.18.turns_ref), channel_id=1, source_target_pairs={{0,32},{32,64},{64,96},{96,128},{128,160},{160,192},{192,224},{224... | collective-permute-start | bytes 49160 | tf_op jit(solution)/shard_map/ppermute | solution.py:497

commit v7 on v6

--- a/solution.py
+++ b/solution.py
@@ -132,30 +132,33 @@
         new = [left * turn_lanes(right, -d) for d in range(1, REACH, 2)]
         return tuple(x + y for x, y in zip(sums, new))
 
+    def with_top_and_ends(t, b, sums):
+        return with_top(t, b, sums[:-5]) + at_ends(t, b, sums[-5:])
+
     def keep(line, value):
         sums_ref[pl.ds(8 * line, 8), :] = value
 
     if top_ref is not None:
-        sums = over_rows(load, count, with_top, 10)
+        sums = over_rows(load, count, with_top_and_ends, 15)
         for h in range(2):
             sums_ref[pl.ds(8 * 24 * h, 48), :] = top_ref[pl.ds(48 * h, 48), :]
             for j in range(1, 6):
                 keep(24 * h + 17 + j, sums[2 * j - 2 + h])
     else:
-        sums = over_rows(load, count, with_top, 22)
+        sums = over_rows(load, count, with_top_and_ends, 27)
         for h in range(2):
             keep(24 * h, sums[h])
             for j in range(1, 6):
                 keep(24 * h + j, sums[4 * j - 2 + h])
                 keep(24 * h + 17 + j, sums[4 * j + h])
+    odd_sums = sums[-5:]
     sums = over_rows(load, count, with_bottom, 24)
     for h in range(2):
         for j in range(6):
             keep(24 * h + 6 + j, sums[4 * j + h])
             keep(24 * h + 12 + j, sums[4 * j + 2 + h])
-    sums = over_rows(load, count, at_ends, 5)
     for j in range(5):
-        keep(LINES + j, sums[j])
+        keep(LINES + j, odd_sums[j])
     for line in (WIDE, LINES - 1, LINES + 5, LINES + 6, LINES + 7):
         keep(line, jnp.zeros((8, 128), f32))
     parts = [sums_ref[pl.ds(k, LINES + 8, stride=8), :] for k in range(8)]
@@ -179,7 +182,7 @@
     low, high = band[:24], band[24:]
     blank = jnp.zeros((1, HALF), f32)
     for block in range(4):
-        for line in (0, DIAGS - 2, DIAGS - 1):
+        for line in (0, 1, DIAGS - 1):
             x_ref[block, line : line + 1, :] = blank
     TT, TB, BT, BB = 0, 1, 2, 3
 

time: 88.6 us -> 92.3 us (1.042)
  Pallas kernels: 11.1 us -> 14.8 us
    pallas_call x5, Pallas kernels: 11.1 us -> 14.8 us  [call(): pl.pallas_call(body, out_shape=shapes, in_specs=[vmem] * len(args), out_s...]
where the time goes in v7:
time: 92.3 us; the launch traced here: 91.9 us
  blocking collectives  54.8 us (59%)
  Pallas kernels  14.8 us (16%)
  starting transfers between devices  12.2 us (13%)
  waiting for transfers between devices  8.93 us (10%)
  local copies, waits for them, and re-layouts  1.07 us (1%)
    all_to_all x2, blocking collectives, exchanged(): return lax.all_to_all(again, far, 0, 0, tiled=True)  45.7 us
    pallas_call x5, Pallas kernels, call(): pl.pallas_call(body, out_shape=shapes, in_specs=[vmem] * len(args), out_s...  14.8 us
    all_to_all x1, blocking collectives, exchanged(): arrived = lax.all_to_all(parts, near, 0, 0, tiled=True)  9.1 us
    all_to_all x1, starting transfers between devices, exchanged(): arrived = lax.all_to_all(parts, near, 0, 0, tiled=True)  8.36 us
    all_to_all x1, waiting for transfers between devices, exchanged(): arrived = lax.all_to_all(parts, near, 0, 0, tiled=True)  7.52 us
    ppermute x1, starting transfers between devices, per_device(): raw = lax.ppermute(snapshots, 'grp', onward)  1.92 us
    ppermute x1, starting transfers between devices, per_device(): their_turns = lax.ppermute(turns, 'grp', onward)  1.92 us
  transfers between devices with their start and end apart: 3, of which 2 were waited for; matrix products, arithmetic and copies ran while one was open for 0% of the time, Pallas kernels for 3%

profile of v7, /device:TPU:8, one launch (start us, length us, event | category | flops | bytes accessed | tf_op | source)
XLA Modules:
  0.0 91.9 jit_solution(14021655472397233248)
XLA Ops:
  0.0 0.0 copy-start
  0.0 1.0 %copy-done = f32[256,512]{1,0:T(8,128)S(1)} copy-done((f32[256,512]{1,0:T(8,128)S(1)}, f32[256,512]{1,0:T(8,128)}, u32[]{:S(2)}) %copy-start) | copy-done | bytes 524312
  1.0 0.0 copy-start.1
  1.0 4.3 %shard_map.17 = (f32[8,48,128]{2,1,0:T(8,128)}, f32[256,256]{1,0:T(8,128)S(1)}) custom-call(f32[256,512]{1,0:T(8,128)S(1)} %copy-done), custom_call_target="tpu_custom_call" | custom-call | tf_op jit(solution)/shard_map/pallas_call | solution.py:457
  5.4 8.4 %all-to-all-start = ((f32[8,48,128]{2,1,0:T(8,128)}), f32[8,48,128]{2,1,0:T(8,128)S(1)}, u32[]{:S(2)}, u32[]{:S(2)}) async-start(f32[8,48,128]{2,1,0:T(8,128)} %get-tuple-element.11), calls=%async_computation | async-start | bytes 393216 | tf_op jit(solution)/shard_map/all_to_all | solution.py:475
  13.7 0.0 copy-done.1
  13.7 1.9 %collective-permute-start.1 = (f32[256,512]{1,0:T(8,128)S(1)}, f32[256,512]{1,0:T(8,128)S(1)}, u32[]{:S(2)}, u32[]{:S(2)}) collective-permute-start(f32[256,512]{1,0:T(8,128)S(1)} %copy-done.1), channel_id=1, source_target_pairs={{0,32},{32,64},{64,96},{96,128},{128,160},{160,192},{192,224},{224... | collective-permute-start | bytes 1572872 | tf_op jit(solution)/shard_map/ppermute | solution.py:497
  15.7 7.5 %all-to-all-done = f32[8,48,128]{2,1,0:T(8,128)S(1)} async-done(((f32[8,48,128]{2,1,0:T(8,128)}), f32[8,48,128]{2,1,0:T(8,128)S(1)}, u32[]{:S(2)}, u32[]{:S(2)}) %all-to-all-start) | async-done | bytes 196640 | tf_op jit(solution)/shard_map/all_to_all | solution.py:475
  23.2 25.5 %all_to_all.20.parts_ref = f32[4,48,128]{2,1,0:T(8,128)S(1)} all-to-all(f32[4,48,128]{2,1,0:T(8,128)S(1)} %broadcast_in_dim.17), channel_id=1, replica_groups=mesh['grp'=16,'z3'=2,'z2'=2,'z1'=2,'z0'=2,'side'=2] {'z3','z2'}, dimensions={0} | all-to-all | bytes 196608 | tf_op jit(solution)/shard_map/all_to_all | solution.py:480
  48.7 1.2 %shard_map.18.turns_ref = f32[16,256]{1,0:T(8,128)S(1)} custom-call(f32[4,48,128]{2,1,0:T(8,128)S(1)} %all_to_all.20.parts_ref), custom_call_target="tpu_custom_call" | custom-call | tf_op jit(solution)/shard_map/pallas_call | solution.py:457
  49.9 1.9 %collective-permute-start = (f32[16,256]{1,0:T(8,128)S(1)}, f32[16,256]{1,0:T(8,128)S(1)}, u32[]{:S(2)}, u32[]{:S(2)}) collective-permute-start(f32[16,256]{1,0:T(8,128)S(1)} %shard_map.18.turns_ref), channel_id=1, source_target_pairs={{0,32},{32,64},{64,96},{96,128},{128,160},{160,192},{192,224},{224... | collective-permute-start | bytes 49160 | tf_op jit(solution)/shard_map/ppermute | solution.py:500
  51.8 1.7 %shard_map.19 = (f32[256,256]{1,0:T(8,128)S(1)}, f32[96,128]{1,0:T(8,128)S(1)}) custom-call(f32[16,256]{1,0:T(8,128)S(1)} %shard_map.18.turns_ref, f32[256,512]{1,0:T(8,128)S(1)} %copy-done.1, f32[256,256]{1,0:T(8,128)S(1)} %get-tuple-element.12.b_ref), custom_call_target="tpu_custom_call" | custom-call | tf_op jit(solution)/shard_map/pallas_call | solution.py:457
  53.5 0.0 collective-permute-done.1.p_ref
  53.5 1.4 %collective-permute-done.turns_ref = f32[16,256]{1,0:T(8,128)S(1)} collective-permute-done((f32[16,256]{1,0:T(8,128)S(1)}, f32[16,256]{1,0:T(8,128)S(1)}, u32[]{:S(2)}, u32[]{:S(2)}) %collective-permute-start) | collective-permute-done | bytes 16416 | tf_op jit(solution)/shard_map/ppermute | solution.py:500
  54.9 4.8 %shard_map.20 = (f32[256,256]{1,0:T(8,128)S(1)}, f32[4,48,128]{2,1,0:T(8,128)S(1)}) custom-call(f32[16,256]{1,0:T(8,128)S(1)} %collective-permute-done.turns_ref, f32[256,512]{1,0:T(8,128)S(1)} %collective-permute-done.1.p_ref, f32[256,256]{1,0:T(8,128)S(1)} %get-tuple-element.13.t_ref, f32[96,128]{1,0:T(8,128)S(1)} %get-tuple-element.14.top_ref), custom_call_target="tpu_custom_call" | custom-call | tf_op jit(solution)/shard_map/pallas_call | solution.py:457
  59.7 9.1 %all_to_all.21 = f32[4,48,128]{2,1,0:T(8,128)S(1)} all-to-all(f32[4,48,128]{2,1,0:T(8,128)S(1)} %get-tuple-element.15), channel_id=1, replica_groups=mesh['grp'=16,'z3'=2,'z2'=2,'z1'=2,'z0'=2,'side'=2] {'z0','side'}, dimensions={0} | all-to-all | bytes 196608 | tf_op jit(solution)/shard_map/all_to_all | solution.py:475
  68.8 20.2 %all_to_all.22.parts_ref = f32[8,48,128]{2,1,0:T(8,128)S(1)} all-to-all(f32[8,48,128]{2,1,0:T(8,128)S(1)} %broadcast_in_dim.19), channel_id=1, replica_groups=mesh['grp'=16,'z3'=2,'z2'=2,'z1'=2,'z0'=2,'side'=2] {'z3','z2','z1'}, dimensions={0} | all-to-all | bytes 393216 | tf_op jit(solution)/shard_map/all_to_all | solution.py:480
  89.0 2.8 %shard_map.21 = f32[256,512]{1,0:T(8,128)} custom-call(f32[8,48,128]{2,1,0:T(8,128)S(1)} %all_to_all.22.parts_ref, f32[256,256]{1,0:T(8,128)S(1)} %get-tuple-element.13.t_ref, f32[256,256]{1,0:T(8,128)S(1)} %get-tuple-element.16.b_ref), custom_call_target="tpu_custom_call" | custom-call | tf_op jit(solution)/shard_map/pallas_call | solution.py:457
  (4 shorter events, 0.0 us)
Async XLA Ops:
  0.0 1.0 %copy-start = (f32[256,512]{1,0:T(8,128)S(1)}, f32[256,512]{1,0:T(8,128)}, u32[]{:S(2)}) copy-start(f32[256,512]{1,0:T(8,128)} %p_ref.3) | copy-start | bytes 1572868
  1.0 12.7 %copy-start.1 = (f32[256,512]{1,0:T(8,128)S(1)}, f32[256,512]{1,0:T(8,128)}, u32[]{:S(2)}) copy-start(f32[256,512]{1,0:T(8,128)} %p_ref.3) | copy-start | bytes 1572868
  5.4 17.8 %all-to-all-start = ((f32[8,48,128]{2,1,0:T(8,128)}), f32[8,48,128]{2,1,0:T(8,128)S(1)}, u32[]{:S(2)}, u32[]{:S(2)}) async-start(f32[8,48,128]{2,1,0:T(8,128)} %get-tuple-element.11), calls=%async_computation | async-start | bytes 393216 | tf_op jit(solution)/shard_map/all_to_all | solution.py:475
  13.7 39.8 %collective-permute-start.1 = (f32[256,512]{1,0:T(8,128)S(1)}, f32[256,512]{1,0:T(8,128)S(1)}, u32[]{:S(2)}, u32[]{:S(2)}) collective-permute-start(f32[256,512]{1,0:T(8,128)S(1)} %copy-done.1), channel_id=1, source_target_pairs={{0,32},{32,64},{64,96},{96,128},{128,160},{160,192},{192,224},{224... | collective-permute-start | bytes 1572872 | tf_op jit(solution)/shard_map/ppermute | solution.py:497
  49.9 5.1 %collective-permute-start = (f32[16,256]{1,0:T(8,128)S(1)}, f32[16,256]{1,0:T(8,128)S(1)}, u32[]{:S(2)}, u32[]{:S(2)}) collective-permute-start(f32[16,256]{1,0:T(8,128)S(1)} %shard_map.18.turns_ref), channel_id=1, source_target_pairs={{0,32},{32,64},{64,96},{96,128},{128,160},{160,192},{192,224},{224... | collective-permute-start | bytes 49160 | tf_op jit(solution)/shard_map/ppermute | solution.py:500

commit v8 on v6

--- a/solution.py
+++ b/solution.py
@@ -89,9 +89,9 @@
     return ref[at, :128], ref[at, 128:256]
 
 
-def over_rows(load, count, step, n):
+def over_rows(load, count, step, n, unroll=16):
     zeros = (jnp.zeros((8, 128), f32),) * n
-    return lax.fori_loop(0, count, lambda k, sums: step(*load(k), sums), zeros, unroll=16)
+    return lax.fori_loop(0, count, lambda k, sums: step(*load(k), sums), zeros, unroll=unroll)
 
 
 def top_band_of(load, count, top_ref):
@@ -119,9 +119,9 @@
                 new += [b[h] * shifted[h] for h in range(2)]
         return tuple(x + y for x, y in zip(sums, new))
 
-    def with_bottom(t, b, sums):
+    def with_bottom(t, b, sums, low=0):
         new = []
-        for d in range(0, REACH + 1, 2):
+        for d in range(low, low + 5, 2):
             shifted = ahead(b, d) if d else b
             for left in (b, t):
                 new += [left[h] * shifted[h] for h in range(2)]
@@ -148,7 +148,8 @@
             for j in range(1, 6):
                 keep(24 * h + j, sums[4 * j - 2 + h])
                 keep(24 * h + 17 + j, sums[4 * j + h])
-    sums = over_rows(load, count, with_bottom, 24)
+    sums = over_rows(load, count, with_bottom, 12, 32)
+    sums += over_rows(load, count, lambda t, b, sums: with_bottom(t, b, sums, 6), 12, 32)
     for h in range(2):
         for j in range(6):
             keep(24 * h + 6 + j, sums[4 * j + h])
@@ -179,7 +180,7 @@
     low, high = band[:24], band[24:]
     blank = jnp.zeros((1, HALF), f32)
     for block in range(4):
-        for line in (0, DIAGS - 2, DIAGS - 1):
+        for line in (0, 1, DIAGS - 1):
             x_ref[block, line : line + 1, :] = blank
     TT, TB, BT, BB = 0, 1, 2, 3
 

time: 88.6 us -> 88.4 us (level)
  no operation moved by 1% of the time
where the time goes in v8:
time: 88.4 us; the launch traced here: 88 us
  blocking collectives  54.8 us (62%)
  starting transfers between devices  12.2 us (14%)
  Pallas kernels  11 us (12%)
  waiting for transfers between devices  8.93 us (10%)
  local copies, waits for them, and re-layouts  1.07 us (1%)
    all_to_all x2, blocking collectives, exchanged(): return lax.all_to_all(again, far, 0, 0, tiled=True)  45.7 us
    pallas_call x5, Pallas kernels, call(): pl.pallas_call(body, out_shape=shapes, in_specs=[vmem] * len(args), out_s...  11 us
    all_to_all x1, blocking collectives, exchanged(): arrived = lax.all_to_all(parts, near, 0, 0, tiled=True)  9.1 us
    all_to_all x1, starting transfers between devices, exchanged(): arrived = lax.all_to_all(parts, near, 0, 0, tiled=True)  8.36 us
    all_to_all x1, waiting for transfers between devices, exchanged(): arrived = lax.all_to_all(parts, near, 0, 0, tiled=True)  7.52 us
    ppermute x1, starting transfers between devices, per_device(): their_turns = lax.ppermute(turns, 'grp', onward)  1.92 us
    ppermute x1, starting transfers between devices, per_device(): raw = lax.ppermute(snapshots, 'grp', onward)  1.92 us
  transfers between devices with their start and end apart: 3, of which 2 were waited for; matrix products, arithmetic and copies ran while one was open for 0% of the time, Pallas kernels for 3%

profile of v8, /device:TPU:8, one launch (start us, length us, event | category | flops | bytes accessed | tf_op | source)
XLA Modules:
  0.0 88.0 jit_solution(2741109778258634483)
XLA Ops:
  0.0 0.0 copy-start
  0.0 1.0 %copy-done = f32[256,512]{1,0:T(8,128)S(1)} copy-done((f32[256,512]{1,0:T(8,128)S(1)}, f32[256,512]{1,0:T(8,128)}, u32[]{:S(2)}) %copy-start) | copy-done | bytes 524312
  1.0 0.0 copy-start.1
  1.0 2.4 %shard_map.17 = (f32[8,48,128]{2,1,0:T(8,128)}, f32[256,256]{1,0:T(8,128)S(1)}) custom-call(f32[256,512]{1,0:T(8,128)S(1)} %copy-done), custom_call_target="tpu_custom_call" | custom-call | tf_op jit(solution)/shard_map/pallas_call | solution.py:455
  3.4 8.4 %all-to-all-start = ((f32[8,48,128]{2,1,0:T(8,128)}), f32[8,48,128]{2,1,0:T(8,128)S(1)}, u32[]{:S(2)}, u32[]{:S(2)}) async-start(f32[8,48,128]{2,1,0:T(8,128)} %get-tuple-element.11), calls=%async_computation | async-start | bytes 393216 | tf_op jit(solution)/shard_map/all_to_all | solution.py:473
  11.8 0.0 copy-done.1
  11.8 1.9 %collective-permute-start.1 = (f32[256,512]{1,0:T(8,128)S(1)}, f32[256,512]{1,0:T(8,128)S(1)}, u32[]{:S(2)}, u32[]{:S(2)}) collective-permute-start(f32[256,512]{1,0:T(8,128)S(1)} %copy-done.1), channel_id=1, source_target_pairs={{0,32},{32,64},{64,96},{96,128},{128,160},{160,192},{192,224},{224... | collective-permute-start | bytes 1572872 | tf_op jit(solution)/shard_map/ppermute | solution.py:495
  13.7 7.5 %all-to-all-done = f32[8,48,128]{2,1,0:T(8,128)S(1)} async-done(((f32[8,48,128]{2,1,0:T(8,128)}), f32[8,48,128]{2,1,0:T(8,128)S(1)}, u32[]{:S(2)}, u32[]{:S(2)}) %all-to-all-start) | async-done | bytes 196640 | tf_op jit(solution)/shard_map/all_to_all | solution.py:473
  21.3 25.5 %all_to_all.20.parts_ref = f32[4,48,128]{2,1,0:T(8,128)S(1)} all-to-all(f32[4,48,128]{2,1,0:T(8,128)S(1)} %broadcast_in_dim.17), channel_id=1, replica_groups=mesh['grp'=16,'z3'=2,'z2'=2,'z1'=2,'z0'=2,'side'=2] {'z3','z2'}, dimensions={0} | all-to-all | bytes 196608 | tf_op jit(solution)/shard_map/all_to_all | solution.py:478
  46.8 1.2 %shard_map.18.turns_ref = f32[16,256]{1,0:T(8,128)S(1)} custom-call(f32[4,48,128]{2,1,0:T(8,128)S(1)} %all_to_all.20.parts_ref), custom_call_target="tpu_custom_call" | custom-call | tf_op jit(solution)/shard_map/pallas_call | solution.py:455
  47.9 1.9 %collective-permute-start = (f32[16,256]{1,0:T(8,128)S(1)}, f32[16,256]{1,0:T(8,128)S(1)}, u32[]{:S(2)}, u32[]{:S(2)}) collective-permute-start(f32[16,256]{1,0:T(8,128)S(1)} %shard_map.18.turns_ref), channel_id=1, source_target_pairs={{0,32},{32,64},{64,96},{96,128},{128,160},{160,192},{192,224},{224... | collective-permute-start | bytes 49160 | tf_op jit(solution)/shard_map/ppermute | solution.py:498
  49.8 1.7 %shard_map.19 = (f32[256,256]{1,0:T(8,128)S(1)}, f32[96,128]{1,0:T(8,128)S(1)}) custom-call(f32[16,256]{1,0:T(8,128)S(1)} %shard_map.18.turns_ref, f32[256,512]{1,0:T(8,128)S(1)} %copy-done.1, f32[256,256]{1,0:T(8,128)S(1)} %get-tuple-element.12.b_ref), custom_call_target="tpu_custom_call" | custom-call | tf_op jit(solution)/shard_map/pallas_call | solution.py:455
  51.6 0.0 collective-permute-done.1.p_ref
  51.6 1.4 %collective-permute-done.turns_ref = f32[16,256]{1,0:T(8,128)S(1)} collective-permute-done((f32[16,256]{1,0:T(8,128)S(1)}, f32[16,256]{1,0:T(8,128)S(1)}, u32[]{:S(2)}, u32[]{:S(2)}) %collective-permute-start) | collective-permute-done | bytes 16416 | tf_op jit(solution)/shard_map/ppermute | solution.py:498
  53.0 2.9 %shard_map.20 = (f32[256,256]{1,0:T(8,128)S(1)}, f32[4,48,128]{2,1,0:T(8,128)S(1)}) custom-call(f32[16,256]{1,0:T(8,128)S(1)} %collective-permute-done.turns_ref, f32[256,512]{1,0:T(8,128)S(1)} %collective-permute-done.1.p_ref, f32[256,256]{1,0:T(8,128)S(1)} %get-tuple-element.13.t_ref, f32[96,128]{1,0:T(8,128)S(1)} %get-tuple-element.14.top_ref), custom_call_target="tpu_custom_call" | custom-call | tf_op jit(solution)/shard_map/pallas_call | solution.py:455
  55.8 9.1 %all_to_all.21 = f32[4,48,128]{2,1,0:T(8,128)S(1)} all-to-all(f32[4,48,128]{2,1,0:T(8,128)S(1)} %get-tuple-element.15), channel_id=1, replica_groups=mesh['grp'=16,'z3'=2,'z2'=2,'z1'=2,'z0'=2,'side'=2] {'z0','side'}, dimensions={0} | all-to-all | bytes 196608 | tf_op jit(solution)/shard_map/all_to_all | solution.py:473
  65.0 20.2 %all_to_all.22.parts_ref = f32[8,48,128]{2,1,0:T(8,128)S(1)} all-to-all(f32[8,48,128]{2,1,0:T(8,128)S(1)} %broadcast_in_dim.19), channel_id=1, replica_groups=mesh['grp'=16,'z3'=2,'z2'=2,'z1'=2,'z0'=2,'side'=2] {'z3','z2','z1'}, dimensions={0} | all-to-all | bytes 393216 | tf_op jit(solution)/shard_map/all_to_all | solution.py:478
  85.2 2.8 %shard_map.21 = f32[256,512]{1,0:T(8,128)} custom-call(f32[8,48,128]{2,1,0:T(8,128)S(1)} %all_to_all.22.parts_ref, f32[256,256]{1,0:T(8,128)S(1)} %get-tuple-element.13.t_ref, f32[256,256]{1,0:T(8,128)S(1)} %get-tuple-element.16.b_ref), custom_call_target="tpu_custom_call" | custom-call | tf_op jit(solution)/shard_map/pallas_call | solution.py:455
  (4 shorter events, 0.0 us)
Async XLA Ops:
  0.0 1.0 %copy-start = (f32[256,512]{1,0:T(8,128)S(1)}, f32[256,512]{1,0:T(8,128)}, u32[]{:S(2)}) copy-start(f32[256,512]{1,0:T(8,128)} %p_ref.3) | copy-start | bytes 1572868
  1.0 10.8 %copy-start.1 = (f32[256,512]{1,0:T(8,128)S(1)}, f32[256,512]{1,0:T(8,128)}, u32[]{:S(2)}) copy-start(f32[256,512]{1,0:T(8,128)} %p_ref.3) | copy-start | bytes 1572868
  3.4 17.8 %all-to-all-start = ((f32[8,48,128]{2,1,0:T(8,128)}), f32[8,48,128]{2,1,0:T(8,128)S(1)}, u32[]{:S(2)}, u32[]{:S(2)}) async-start(f32[8,48,128]{2,1,0:T(8,128)} %get-tuple-element.11), calls=%async_computation | async-start | bytes 393216 | tf_op jit(solution)/shard_map/all_to_all | solution.py:473
  11.8 39.8 %collective-permute-start.1 = (f32[256,512]{1,0:T(8,128)S(1)}, f32[256,512]{1,0:T(8,128)S(1)}, u32[]{:S(2)}, u32[]{:S(2)}) collective-permute-start(f32[256,512]{1,0:T(8,128)S(1)} %copy-done.1), channel_id=1, source_target_pairs={{0,32},{32,64},{64,96},{96,128},{128,160},{160,192},{192,224},{224... | collective-permute-start | bytes 1572872 | tf_op jit(solution)/shard_map/ppermute | solution.py:495
  47.9 5.1 %collective-permute-start = (f32[16,256]{1,0:T(8,128)S(1)}, f32[16,256]{1,0:T(8,128)S(1)}, u32[]{:S(2)}, u32[]{:S(2)}) collective-permute-start(f32[16,256]{1,0:T(8,128)S(1)} %shard_map.18.turns_ref), channel_id=1, source_target_pairs={{0,32},{32,64},{64,96},{96,128},{128,160},{160,192},{192,224},{224... | collective-permute-start | bytes 49160 | tf_op jit(solution)/shard_map/ppermute | solution.py:498

commit v9 on v8

--- a/solution.py
+++ b/solution.py
@@ -136,7 +136,7 @@
         sums_ref[pl.ds(8 * line, 8), :] = value
 
     if top_ref is not None:
-        sums = over_rows(load, count, with_top, 10)
+        sums = over_rows(load, count, with_top, 10, 32)
         for h in range(2):
             sums_ref[pl.ds(8 * 24 * h, 48), :] = top_ref[pl.ds(48 * h, 48), :]
             for j in range(1, 6):

time: 88.4 us -> 88.2 us (level)
  no operation moved by 1% of the time
where the time goes in v9:
time: 88.2 us; the launch traced here: 87.8 us
  blocking collectives  54.8 us (62%)
  starting transfers between devices  12.2 us (14%)
  Pallas kernels  10.8 us (12%)
  waiting for transfers between devices  8.93 us (10%)
  local copies, waits for them, and re-layouts  1.07 us (1%)
    all_to_all x2, blocking collectives, exchanged(): return lax.all_to_all(again, far, 0, 0, tiled=True)  45.7 us
    pallas_call x5, Pallas kernels, call(): pl.pallas_call(body, out_shape=shapes, in_specs=[vmem] * len(args), out_s...  10.8 us
    all_to_all x1, blocking collectives, exchanged(): arrived = lax.all_to_all(parts, near, 0, 0, tiled=True)  9.1 us
    all_to_all x1, starting transfers between devices, exchanged(): arrived = lax.all_to_all(parts, near, 0, 0, tiled=True)  8.36 us
    all_to_all x1, waiting for transfers between devices, exchanged(): arrived = lax.all_to_all(parts, near, 0, 0, tiled=True)  7.52 us
    ppermute x1, starting transfers between devices, per_device(): raw = lax.ppermute(snapshots, 'grp', onward)  1.92 us
    ppermute x1, starting transfers between devices, per_device(): their_turns = lax.ppermute(turns, 'grp', onward)  1.92 us
  transfers between devices with their start and end apart: 3, of which 2 were waited for; matrix products, arithmetic and copies ran while one was open for 0% of the time, Pallas kernels for 3%

profile of v9, /device:TPU:8, one launch (start us, length us, event | category | flops | bytes accessed | tf_op | source)
XLA Modules:
  0.0 87.8 jit_solution(10923268877019353395)
XLA Ops:
  0.0 0.0 copy-start
  0.0 1.0 %copy-done = f32[256,512]{1,0:T(8,128)S(1)} copy-done((f32[256,512]{1,0:T(8,128)S(1)}, f32[256,512]{1,0:T(8,128)}, u32[]{:S(2)}) %copy-start) | copy-done | bytes 524312
  1.0 0.0 copy-start.1
  1.0 2.4 %shard_map.17 = (f32[8,48,128]{2,1,0:T(8,128)}, f32[256,256]{1,0:T(8,128)S(1)}) custom-call(f32[256,512]{1,0:T(8,128)S(1)} %copy-done), custom_call_target="tpu_custom_call" | custom-call | tf_op jit(solution)/shard_map/pallas_call | solution.py:455
  3.4 8.4 %all-to-all-start = ((f32[8,48,128]{2,1,0:T(8,128)}), f32[8,48,128]{2,1,0:T(8,128)S(1)}, u32[]{:S(2)}, u32[]{:S(2)}) async-start(f32[8,48,128]{2,1,0:T(8,128)} %get-tuple-element.11), calls=%async_computation | async-start | bytes 393216 | tf_op jit(solution)/shard_map/all_to_all | solution.py:473
  11.8 0.0 copy-done.1
  11.8 1.9 %collective-permute-start.1 = (f32[256,512]{1,0:T(8,128)S(1)}, f32[256,512]{1,0:T(8,128)S(1)}, u32[]{:S(2)}, u32[]{:S(2)}) collective-permute-start(f32[256,512]{1,0:T(8,128)S(1)} %copy-done.1), channel_id=1, source_target_pairs={{0,32},{32,64},{64,96},{96,128},{128,160},{160,192},{192,224},{224... | collective-permute-start | bytes 1572872 | tf_op jit(solution)/shard_map/ppermute | solution.py:495
  13.7 7.5 %all-to-all-done = f32[8,48,128]{2,1,0:T(8,128)S(1)} async-done(((f32[8,48,128]{2,1,0:T(8,128)}), f32[8,48,128]{2,1,0:T(8,128)S(1)}, u32[]{:S(2)}, u32[]{:S(2)}) %all-to-all-start) | async-done | bytes 196640 | tf_op jit(solution)/shard_map/all_to_all | solution.py:473
  21.3 25.5 %all_to_all.20.parts_ref = f32[4,48,128]{2,1,0:T(8,128)S(1)} all-to-all(f32[4,48,128]{2,1,0:T(8,128)S(1)} %broadcast_in_dim.17), channel_id=1, replica_groups=mesh['grp'=16,'z3'=2,'z2'=2,'z1'=2,'z0'=2,'side'=2] {'z3','z2'}, dimensions={0} | all-to-all | bytes 196608 | tf_op jit(solution)/shard_map/all_to_all | solution.py:478
  46.8 1.2 %shard_map.18.turns_ref = f32[16,256]{1,0:T(8,128)S(1)} custom-call(f32[4,48,128]{2,1,0:T(8,128)S(1)} %all_to_all.20.parts_ref), custom_call_target="tpu_custom_call" | custom-call | tf_op jit(solution)/shard_map/pallas_call | solution.py:455
  47.9 1.9 %collective-permute-start = (f32[16,256]{1,0:T(8,128)S(1)}, f32[16,256]{1,0:T(8,128)S(1)}, u32[]{:S(2)}, u32[]{:S(2)}) collective-permute-start(f32[16,256]{1,0:T(8,128)S(1)} %shard_map.18.turns_ref), channel_id=1, source_target_pairs={{0,32},{32,64},{64,96},{96,128},{128,160},{160,192},{192,224},{224... | collective-permute-start | bytes 49160 | tf_op jit(solution)/shard_map/ppermute | solution.py:498
  49.8 1.7 %shard_map.19 = (f32[256,256]{1,0:T(8,128)S(1)}, f32[96,128]{1,0:T(8,128)S(1)}) custom-call(f32[16,256]{1,0:T(8,128)S(1)} %shard_map.18.turns_ref, f32[256,512]{1,0:T(8,128)S(1)} %copy-done.1, f32[256,256]{1,0:T(8,128)S(1)} %get-tuple-element.12.b_ref), custom_call_target="tpu_custom_call" | custom-call | tf_op jit(solution)/shard_map/pallas_call | solution.py:455
  51.6 0.0 collective-permute-done.1.p_ref
  51.6 1.4 %collective-permute-done.turns_ref = f32[16,256]{1,0:T(8,128)S(1)} collective-permute-done((f32[16,256]{1,0:T(8,128)S(1)}, f32[16,256]{1,0:T(8,128)S(1)}, u32[]{:S(2)}, u32[]{:S(2)}) %collective-permute-start) | collective-permute-done | bytes 16416 | tf_op jit(solution)/shard_map/ppermute | solution.py:498
  53.0 2.7 %shard_map.20 = (f32[256,256]{1,0:T(8,128)S(1)}, f32[4,48,128]{2,1,0:T(8,128)S(1)}) custom-call(f32[16,256]{1,0:T(8,128)S(1)} %collective-permute-done.turns_ref, f32[256,512]{1,0:T(8,128)S(1)} %collective-permute-done.1.p_ref, f32[256,256]{1,0:T(8,128)S(1)} %get-tuple-element.13.t_ref, f32[96,128]{1,0:T(8,128)S(1)} %get-tuple-element.14.top_ref), custom_call_target="tpu_custom_call" | custom-call | tf_op jit(solution)/shard_map/pallas_call | solution.py:455
  55.6 9.1 %all_to_all.21 = f32[4,48,128]{2,1,0:T(8,128)S(1)} all-to-all(f32[4,48,128]{2,1,0:T(8,128)S(1)} %get-tuple-element.15), channel_id=1, replica_groups=mesh['grp'=16,'z3'=2,'z2'=2,'z1'=2,'z0'=2,'side'=2] {'z0','side'}, dimensions={0} | all-to-all | bytes 196608 | tf_op jit(solution)/shard_map/all_to_all | solution.py:473
  64.8 20.2 %all_to_all.22.parts_ref = f32[8,48,128]{2,1,0:T(8,128)S(1)} all-to-all(f32[8,48,128]{2,1,0:T(8,128)S(1)} %broadcast_in_dim.19), channel_id=1, replica_groups=mesh['grp'=16,'z3'=2,'z2'=2,'z1'=2,'z0'=2,'side'=2] {'z3','z2','z1'}, dimensions={0} | all-to-all | bytes 393216 | tf_op jit(solution)/shard_map/all_to_all | solution.py:478
  85.0 2.8 %shard_map.21 = f32[256,512]{1,0:T(8,128)} custom-call(f32[8,48,128]{2,1,0:T(8,128)S(1)} %all_to_all.22.parts_ref, f32[256,256]{1,0:T(8,128)S(1)} %get-tuple-element.13.t_ref, f32[256,256]{1,0:T(8,128)S(1)} %get-tuple-element.16.b_ref), custom_call_target="tpu_custom_call" | custom-call | tf_op jit(solution)/shard_map/pallas_call | solution.py:455
  (4 shorter events, 0.0 us)
Async XLA Ops:
  0.0 1.0 %copy-start = (f32[256,512]{1,0:T(8,128)S(1)}, f32[256,512]{1,0:T(8,128)}, u32[]{:S(2)}) copy-start(f32[256,512]{1,0:T(8,128)} %p_ref.3) | copy-start | bytes 1572868
  1.0 10.8 %copy-start.1 = (f32[256,512]{1,0:T(8,128)S(1)}, f32[256,512]{1,0:T(8,128)}, u32[]{:S(2)}) copy-start(f32[256,512]{1,0:T(8,128)} %p_ref.3) | copy-start | bytes 1572868
  3.4 17.8 %all-to-all-start = ((f32[8,48,128]{2,1,0:T(8,128)}), f32[8,48,128]{2,1,0:T(8,128)S(1)}, u32[]{:S(2)}, u32[]{:S(2)}) async-start(f32[8,48,128]{2,1,0:T(8,128)} %get-tuple-element.11), calls=%async_computation | async-start | bytes 393216 | tf_op jit(solution)/shard_map/all_to_all | solution.py:473
  11.8 39.8 %collective-permute-start.1 = (f32[256,512]{1,0:T(8,128)S(1)}, f32[256,512]{1,0:T(8,128)S(1)}, u32[]{:S(2)}, u32[]{:S(2)}) collective-permute-start(f32[256,512]{1,0:T(8,128)S(1)} %copy-done.1), channel_id=1, source_target_pairs={{0,32},{32,64},{64,96},{96,128},{128,160},{160,192},{192,224},{224... | collective-permute-start | bytes 1572872 | tf_op jit(solution)/shard_map/ppermute | solution.py:495
  47.9 5.1 %collective-permute-start = (f32[16,256]{1,0:T(8,128)S(1)}, f32[16,256]{1,0:T(8,128)S(1)}, u32[]{:S(2)}, u32[]{:S(2)}) collective-permute-start(f32[16,256]{1,0:T(8,128)S(1)} %shard_map.18.turns_ref), channel_id=1, source_target_pairs={{0,32},{32,64},{64,96},{96,128},{128,160},{160,192},{192,224},{224... | collective-permute-start | bytes 49160 | tf_op jit(solution)/shard_map/ppermute | solution.py:498
